TPU v7x, 32 devices: a whole 2x2x4 slice. The times are simulated.
32 devices in a mesh: section: 4 (over y, x), expert: 8 (over z, core).
Axes of the slice: x: 2, y: 2, z: 4, core: 2. Of those that a mesh axis runs over, the one named last changes fastest.
Arguments:
- upstream: bfloat16 [4, 1024, 3584], P('section', 'expert'), may hold values from -0.59765625 to 0.59765625
- routes: int32 [4, 1024, 2], P('section', 'expert'), may hold values from 0 to 7, all different within a row; in each aligned block of 128 rows (0 to 127, 128 to 255, ..., all dimensions but the last counted through in order) at most 48 rows name the same one
- gates: float32 [4, 1024, 2], P('section', 'expert'), may hold values from 0.1 to 1
- w_gate: bfloat16 [4, 3584, 8192], P('section', None, 'expert'), may hold values from -0.09375 to 0.09375
- w_up: bfloat16 [4, 3584, 8192], P('section', None, 'expert'), may hold values from -0.09375 to 0.09375
- w_down: bfloat16 [4, 8192, 3584], P('section', 'expert'), may hold values from -0.1875 to 0.1875
- stash_q: bfloat16 [4, 3072, 3584], P('section', 'expert'), may hold values from -448 to 448
- stash_scale: float32 [4, 3072, 28], P('section', 'expert'), may hold values from 0.004 to 0.04
Outputs:
- grad_input: bfloat16 [4, 1024, 3584], P('section', 'expert')
- grad_gates: float32 [4, 1024, 2], P('section', 'expert')
- grad_w_gate: bfloat16 [4, 3584, 8192], P('section', None, 'expert')
- grad_w_up: bfloat16 [4, 3584, 8192], P('section', None, 'expert')
- grad_w_down: bfloat16 [4, 8192, 3584], P('section', 'expert')
Inputs may be any that keep to these rules, and one draw needn't show every extreme that they name: `routes`: in each section, each token names 2 different experts, and within the 128 tokens of one device no expert is named more than 48 times; some expert is named exactly 48 times.
All inputs are finite; a program needn't handle non-finite values.
Results may differ from a plain program's by a relative error of at most 0.014.
Values may be sent and summed in bfloat16 or wider, within the bound.
No kernel may reach another device: no remote copies, remote signals or barrier semaphores. Data moves between devices by JAX's collectives and lax.ppermute only.
A program may use at most 256 MiB of HBM per device.

v0:
```python
import jax
import jax.numpy as jnp
from jax import lax
from jax.experimental import pallas as pl
from jax.experimental.pallas import tpu as pltpu
from jax.sharding import PartitionSpec as P

EXPERT = "expert"
SECTION = "section"
EXPERTS = 8
CAP = 48
OUT_CUTS = (10, 18)
BACK_CUTS = (10, 18)


def shifted(x, axis, by):
    size = lax.axis_size(axis)
    return lax.ppermute(x, axis, [(i, (i + by) % size) for i in range(size)])


def swap(x, bit):
    return lax.ppermute(x, EXPERT, [(i, i ^ bit) for i in range(8)])


def together(*arrays):
    return lax.optimization_barrier(arrays)


def mm(a, b, dims):
    return lax.dot_general(a, b, (dims, ((), ())), preferred_element_type=jnp.float32)


def stacked(*arrays):
    return jnp.concatenate(arrays, axis=0)


def scale_kernel(order, *refs):
    *pairs, out = refs
    for j in range(len(pairs) // 2):
        codes, scales = pairs[2 * j], pairs[2 * j + 1]
        rows = slice(CAP * j, CAP * (j + 1))
        for b in range(codes.shape[1] // 128):
            at = slice(128 * b, 128 * (b + 1))
            got = codes[:, at].astype(jnp.float32) * scales[:, b : b + 1]
            out[rows, at] = got.astype(out.dtype)


def scaled_blocks(order, codes, scales):
    count, width = codes.shape
    at_once = 4
    specs = []
    for j in range(at_once):
        specs.append(pl.BlockSpec((CAP, width), lambda i, order, j=j: (order[at_once * i + j], 0)))
        specs.append(
            pl.BlockSpec((CAP, scales.shape[1]), lambda i, order, j=j: (order[at_once * i + j], 0))
        )
    return pl.pallas_call(
        scale_kernel,
        grid_spec=pltpu.PrefetchScalarGridSpec(
            num_scalar_prefetch=1,
            grid=(count // CAP // at_once,),
            in_specs=specs,
            out_specs=pl.BlockSpec((CAP * at_once, width), lambda i, order: (i, 0)),
        ),
        out_shape=jax.ShapeDtypeStruct((count, width), jnp.bfloat16),
        compiler_params=pltpu.CompilerParams(vmem_limit_bytes=24 * 2**20),
        cost_estimate=pl.CostEstimate(
            flops=count * width, bytes_accessed=4 * count * width, transcendentals=0
        ),
    )(order, *[codes, scales] * at_once)


def spans_of(width, cuts):
    blocks, total = width // 128, sum(cuts)
    edges = [128 * (blocks * sum(cuts[:j]) // total) for j in range(len(cuts) + 1)]
    return list(zip(edges[:-1], edges[1:]))


def relayed(upstream, routes, gates, w_gate, w_up, w_down, stash_q, stash_scale):
    bf16, f32 = jnp.bfloat16, jnp.float32
    tokens, width = upstream.shape[1], upstream.shape[2]
    spans, steps = spans_of(width, OUT_CUTS), len(OUT_CUTS)
    half = 4 * CAP
    me = lax.axis_index(EXPERT)
    gate_cols, up_cols, down_rows = w_gate[0], w_up[0], w_down[0]
    codes, scales = stash_q[0], stash_scale[0]
    pieces = [upstream[0, :, lo:hi] for lo, hi in spans]
    xs = [shifted(pieces[0], SECTION, -1)]

    route = routes[0].T
    ids = jnp.arange(EXPERTS, dtype=jnp.int32)
    hit = route[:, None, :] == (ids ^ me)[None, :, None]
    named = jnp.any(hit, axis=0)
    earlier = (jnp.arange(tokens)[:, None] < jnp.arange(tokens)[None, :]).astype(bf16)
    plan = jnp.where(named, mm(named.astype(bf16), earlier, ((1,), (0,))), -1.0)
    gate_of = jnp.sum(jnp.where(hit, gates[0].T[:, None, :], 0.0), axis=0)
    slot_ids = jnp.arange(CAP, dtype=f32)[None, :, None]

    def selection(rows):
        return (rows[:, None, :] == slot_ids).astype(bf16).reshape(-1, tokens)

    def traded(name, rows, which):
        got = {}
        for m in which:
            got[m] = swap(rows[CAP * m : CAP * (m + 1)], m)
        return got

    def pack(sel, rows):
        return mm(sel, rows, ((1,), (0,))).astype(bf16)

    def pieces_of(values):
        got = []
        for _ in range(3):
            got.append(lax.reduce_precision(values, 8, 7))
            values = values - got[-1]
        return jnp.stack(got, axis=-1).astype(bf16)

    def gate_columns(table):
        columns = pieces_of(table).transpose(1, 0, 2).reshape(tokens, -1)
        return jnp.pad(columns, ((0, 0), (0, 128 - columns.shape[1])))

    near_sel = selection(plan[:4])
    both = jnp.stack([plan, gate_of])
    x, pieces, near_sel, both, codes, scales = together(
        xs[0], pieces, near_sel, both, codes, scales
    )

    cross = swap(x, 4)
    x1 = shifted(pieces[1], SECTION, -1)
    own = jnp.concatenate([pack(near_sel, x), pack(near_sel, gate_columns(both[1, :4]))], axis=1)
    own, both, codes = together(own, both, codes)
    near_own = swap(own[2 * CAP :], 2)
    far_both = swap(both, 4)
    inputs = scaled_blocks(me ^ jnp.arange(8, dtype=jnp.int32), codes, scales)
    cross, x, own, near_own, far_both, inputs = together(cross, x1, own, near_own, far_both, inputs)

    next_cross = swap(x, 4)
    far_sel = selection(far_both[0, 4:])
    far = [pack(far_sel, cross), pack(far_sel, gate_columns(far_both[1, 4:]))]
    far = jnp.concatenate(far, axis=1)
    far, x, own, near_own, inputs = together(far, x, own, near_own, inputs)
    near_far = swap(far[2 * CAP :], 2)
    own_1 = pack(near_sel, x)
    own_1, own, near_own, inputs = together(own_1, own, near_own, inputs)
    near_own_1 = swap(own_1[2 * CAP :], 2)
    given = swap(stacked(own[CAP : 2 * CAP], near_own[CAP:]), 1)
    gate_pre = mm(inputs, gate_cols, ((1,), (0,)))
    up_pre = mm(inputs, up_cols, ((1,), (0,)))
    near_rows = stacked(own[:CAP], given[:CAP], near_own[:CAP], given[CAP:])
    cross, near_far, near_own_1, near_rows, gate_pre, up_pre, far, own_1 = together(
        next_cross, near_far, near_own_1, near_rows, gate_pre, up_pre, far, own_1
    )

    far_1 = pack(far_sel, cross)
    far_1, far, near_far, own_1, near_own_1, near_rows = together(
        far_1, far, near_far, own_1, near_own_1, near_rows
    )
    got = traded("far_1", far_1, (2, 3, 1))
    given = swap(stacked(far[CAP : 2 * CAP], near_far[CAP:]), 1)
    given_1 = swap(stacked(own_1[CAP : 2 * CAP], near_own_1[CAP:]), 1)
    rows = stacked(near_rows, far[:CAP], given[:CAP], near_far[:CAP], given[CAP:])
    lo = spans[1][0]
    wanted = jnp.arange(128)[None, :] // 3 == jnp.arange(8 * CAP)[:, None] // CAP % 4
    weights = jnp.sum(jnp.where(wanted, rows[:, lo:].astype(f32), 0.0), axis=1, keepdims=True)
    parts = [rows[:, :lo]]
    raw_grad = mm(parts[0], down_rows[:, :lo], ((1,), (1,)))
    sigma = jax.nn.sigmoid(gate_pre)
    swish = gate_pre * sigma
    hidden = swish * up_pre
    scaled_hidden = (weights * hidden).astype(bf16)
    to_gate = weights * up_pre * sigma * (1.0 + gate_pre * (1.0 - sigma))
    to_up = weights * swish
    got, given_1, parts, raw_grad, hidden, scaled_hidden, to_gate, to_up = together(
        got, given_1, parts, raw_grad, hidden, scaled_hidden, to_gate, to_up
    )
    parts.append(
        stacked(
            own_1[:CAP], given_1[:CAP], near_own_1[:CAP], given_1[CAP:], far_1[:CAP], got[1], got[2], got[3]
        )
    )
    raw_grad = raw_grad + mm(parts[1], down_rows[:, lo:], ((1,), (1,)))
    grad_gate_pre = (raw_grad * to_gate).astype(bf16)
    grad_up_pre = (raw_grad * to_up).astype(bf16)

    spans, steps = spans_of(width, BACK_CUTS), len(BACK_CUTS)
    column = jnp.arange(128, dtype=jnp.int32)[None, :]

    def back_of(j, ggp, gup):
        lo, hi = spans[j]
        back = mm(ggp, gate_cols[lo:hi], ((1,), (1,)))
        return (back + mm(gup, up_cols[lo:hi], ((1,), (1,)))).astype(bf16)

    def gate_terms(hidden, raw_grad):
        left = jnp.sum(hidden * raw_grad, axis=1, keepdims=True)
        terms = jnp.zeros((left.shape[0], 128), f32)
        for i in range(3):
            piece = lax.reduce_precision(left, 8, 7)
            terms = jnp.where(column == 3 * me + i, piece, terms)
            left = left - piece
        return terms.astype(bf16)

    def far_hands(j):
        got = traded(f"rfar_{j}", back[j][half:], (2, 3, 1))
        return [back[j][half : half + CAP]] + [got[m] for m in (1, 2, 3)]

    rest = (grad_gate_pre, grad_up_pre, inputs, raw_grad, hidden, scaled_hidden, parts)
    back = {0: back_of(0, grad_gate_pre, grad_up_pre)}
    back[0], rest = together(back[0], rest)
    hands = far_hands(0)
    back[1] = back_of(1, *rest[:2])
    back[1] = jnp.concatenate([back[1], gate_terms(rest[4], rest[3])], axis=1)
    near_back = jnp.concatenate([back[j][:half] for j in range(steps)], axis=1)
    hands, back, rest, near_back = together(hands, back, rest, near_back)

    def crossing(name, hands):
        far_sum = mm(far_sel, stacked(*hands), ((0,), (0,))).astype(bf16)
        return far_sum

    more = far_hands(1)
    far_sum = crossing(0, hands)
    far_sum, rest, near_back = together(far_sum, rest, near_back)
    crossed = [swap(far_sum, 4)]
    near = traded("rnear", near_back, (2,))
    grad_gw = mm(rest[2], rest[0], ((0,), (0,))).astype(bf16)
    hands, grad_gw, rest, near_back = together(more, grad_gw, rest, near_back)
    far_sum = crossing(1, hands)
    far_sum, rest, near_back = together(far_sum, rest, near_back)
    crossed.append(swap(far_sum, 4))
    near.update(traded("rnear", near_back, (3, 1)))
    grad_uw = mm(rest[2], rest[1], ((0,), (0,))).astype(bf16)
    grad_dw = mm(rest[5], jnp.concatenate(rest[6], axis=1), ((0,), (0,))).astype(bf16)
    total = mm(near_sel, stacked(near_back[:CAP], near[1], near[2], near[3]), ((0,), (0,)))
    total = (total + jnp.concatenate(crossed, axis=1).astype(f32)).astype(bf16)
    terms, grad_input = total[:, width:].astype(f32), total[:, :width]
    wanted = column[None] // 3 == routes[0][:, :, None]
    grad_gates = jnp.sum(jnp.where(wanted, terms[:, None, :], 0.0), axis=2)
    return grad_input[None], grad_gates[None], grad_gw[None], grad_uw[None], grad_dw[None]


def slot_work(codes, scales, cotangent, weights, gate_cols, up_cols, down_rows):
    count, width = codes.shape
    blocks = width // 128
    inputs = (
        (codes.astype(jnp.float32).reshape(count, blocks, 128) * scales[:, :, None])
        .reshape(count, width)
        .astype(jnp.bfloat16)
    )
    gate_pre = jnp.dot(inputs, gate_cols, preferred_element_type=jnp.float32)
    up_pre = jnp.dot(inputs, up_cols, preferred_element_type=jnp.float32)
    sigma = jax.nn.sigmoid(gate_pre)
    swish = gate_pre * sigma
    hidden = swish * up_pre
    scaled_hidden = (weights[:, None] * hidden).astype(jnp.bfloat16)
    grad_down = lax.dot_general(
        scaled_hidden, cotangent, (((0,), (0,)), ((), ())), preferred_element_type=jnp.float32
    )
    raw_grad = lax.dot_general(
        cotangent, down_rows, (((1,), (1,)), ((), ())), preferred_element_type=jnp.float32
    )
    gate_part = jnp.sum(hidden * raw_grad, axis=1)
    grad_hidden = weights[:, None] * raw_grad
    grad_gate_pre = (grad_hidden * up_pre * sigma * (1.0 + gate_pre * (1.0 - sigma))).astype(
        jnp.bfloat16
    )
    grad_up_pre = (grad_hidden * swish).astype(jnp.bfloat16)
    grad_gate_w = lax.dot_general(
        inputs, grad_gate_pre, (((0,), (0,)), ((), ())), preferred_element_type=jnp.float32
    )
    grad_up_w = lax.dot_general(
        inputs, grad_up_pre, (((0,), (0,)), ((), ())), preferred_element_type=jnp.float32
    )
    input_sum = lax.dot_general(
        grad_gate_pre, gate_cols, (((1,), (1,)), ((), ())), preferred_element_type=jnp.float32
    )
    input_sum = input_sum + lax.dot_general(
        grad_up_pre, up_cols, (((1,), (1,)), ((), ())), preferred_element_type=jnp.float32
    )
    return (grad_gate_w, grad_up_w, grad_down, input_sum.astype(jnp.bfloat16), gate_part)


def general(upstream, routes, gates, w_gate, w_up, w_down, stash_q, stash_scale):
    cotangent = shifted(upstream[0], SECTION, -1)
    tok_dev = routes.shape[1]
    topk = routes.shape[2]
    width = cotangent.shape[1]
    groups = lax.axis_size(EXPERT)
    hsplit = groups // EXPERTS
    slots = groups * CAP
    flat = routes[0].reshape(-1)
    onehot = (flat[:, None] == jnp.arange(EXPERTS, dtype=jnp.int32)[None, :]).astype(jnp.int32)
    before = jnp.cumsum(onehot, axis=0) - onehot
    slot = jnp.sum(before * onehot, axis=1)
    target = flat * CAP + slot
    token = jnp.arange(tok_dev * topk, dtype=jnp.int32) // topk
    row_buf = jnp.zeros((EXPERTS * CAP, width), jnp.bfloat16).at[target].set(cotangent[token])
    weight_buf = jnp.zeros((EXPERTS * CAP,), jnp.float32).at[target].set(gates[0].reshape(-1))
    send_rows = jnp.repeat(row_buf.reshape(EXPERTS, CAP, width), hsplit, axis=0)
    send_weights = jnp.repeat(weight_buf.reshape(EXPERTS, CAP), hsplit, axis=0)
    got_rows, got_weights = (
        lax.all_to_all(send_rows, EXPERT, split_axis=0, concat_axis=0, tiled=True),
        lax.all_to_all(
            send_weights.astype(jnp.bfloat16), EXPERT, split_axis=0, concat_axis=0, tiled=True
        ).astype(send_weights.dtype),
    )
    rows = got_rows.reshape(slots, width)
    weights = got_weights.reshape(slots)
    grad_gw, grad_uw, grad_dw, input_part, gate_part = slot_work(
        stash_q[0], stash_scale[0], rows, weights, w_gate[0], w_up[0], w_down[0]
    )
    back_rows, back_gates = (
        lax.all_to_all(
            input_part.reshape(groups, CAP, width), EXPERT, split_axis=0, concat_axis=0, tiled=True
        ),
        lax.all_to_all(
            gate_part.reshape(groups, CAP).astype(jnp.bfloat16),
            EXPERT,
            split_axis=0,
            concat_axis=0,
            tiled=True,
        ).astype(jnp.float32),
    )
    summed = jnp.sum(
        back_rows.reshape(EXPERTS, hsplit, CAP, width).astype(jnp.float32), axis=1
    ).reshape(EXPERTS * CAP, width)
    gate_sum = jnp.sum(
        back_gates.reshape(EXPERTS, hsplit, CAP).astype(jnp.float32), axis=1
    ).reshape(EXPERTS * CAP)
    grad_input = jnp.sum(summed[target].reshape(tok_dev, topk, width), axis=1).astype(jnp.bfloat16)
    grad_gates = gate_sum[target].reshape(tok_dev, topk)
    return (
        grad_input[None],
        grad_gates[None],
        grad_gw.astype(jnp.bfloat16)[None],
        grad_uw.astype(jnp.bfloat16)[None],
        grad_dw.astype(jnp.bfloat16)[None],
    )


def solution(mesh):
    return jax.shard_map(
        relayed if mesh.shape[EXPERT] == EXPERTS else general,
        mesh=mesh,
        in_specs=(
            P(SECTION, EXPERT, None),
            P(SECTION, EXPERT, None),
            P(SECTION, EXPERT, None),
            P(SECTION, None, EXPERT),
            P(SECTION, None, EXPERT),
            P(SECTION, EXPERT, None),
            P(SECTION, EXPERT, None),
            P(SECTION, EXPERT, None),
        ),
        out_specs=(
            P(SECTION, EXPERT, None),
            P(SECTION, EXPERT, None),
            P(SECTION, None, EXPERT),
            P(SECTION, None, EXPERT),
            P(SECTION, EXPERT, None),
        ),
        check_vma=False,
    )
```

profile of v0, /device:TPU:0, one launch (start us, length us, event | category | flops | bytes accessed | tf_op | source)
XLA Modules:
  0.0 150.1 jit_solution(11349307301284798090)
XLA Ops:
  1.7 3.9 %collective-permute-start = (bf16[128,1280]{1,0:T(8,128)(2,1)S(1)}, bf16[128,1280]{1,0:T(8,128)(2,1)}, u32[]{:S(2)}, u32[]{:S(2)}) collective-permute-start(bf16[128,1280]{1,0:T(8,128)(2,1)S(1)} %slice_bitcast_fusion.2), channel_id=1, source_target_pairs={{0,24},{8,0},{16,8},{24,16},{1,25},{9,1},{17,9},{25,17},{2,26},{10... | collective-permute-start | bytes 983048 | tf_op jit(solution)/shard_map/ppermute | solution.py:18
  5.6 1.9 %slice_bitcast_fusion.1 = bf16[128,2304]{1,0:T(8,128)(2,1)} fusion(bf16[1,128,3584]{2,1,0:T(8,128)(2,1)} %param.8), kind=kLoop, calls=%fused_computation.70 | loop fusion | bytes 1179648 | tf_op jit(solution)/shard_map/squeeze | solution.py:87
  8.8 3.8 %collective-permute-done = bf16[128,1280]{1,0:T(8,128)(2,1)} collective-permute-done((bf16[128,1280]{1,0:T(8,128)(2,1)S(1)}, bf16[128,1280]{1,0:T(8,128)(2,1)}, u32[]{:S(2)}, u32[]{:S(2)}) %collective-permute-start) | collective-permute-done | bytes 327712 | tf_op jit(solution)/shard_map/ppermute | solution.py:18
  12.6 2.8 %collective-permute-start.1 = (bf16[128,1280]{1,0:T(8,128)(2,1)}, bf16[128,1280]{1,0:T(8,128)(2,1)}, u32[]{:S(2)}, u32[]{:S(2)}) collective-permute-start(bf16[128,1280]{1,0:T(8,128)(2,1)} %collective-permute-done), channel_id=1, source_target_pairs={{0,4},{1,5},{2,6},{3,7},{4,0},{5,1},{6,2},{7,3},{8,12},{9,13},{10,... | collective-permute-start | bytes 983048 | tf_op jit(solution)/shard_map/ppermute | solution.py:22
  16.7 3.4 %collective-permute-start.2 = (bf16[128,2304]{1,0:T(8,128)(2,1)}, bf16[128,2304]{1,0:T(8,128)(2,1)}, u32[]{:S(2)}, u32[]{:S(2)}) collective-permute-start(bf16[128,2304]{1,0:T(8,128)(2,1)} %slice_bitcast_fusion.1), channel_id=1, source_target_pairs={{0,24},{8,0},{16,8},{24,16},{1,25},{9,1},{17,9},{25,17},{2,26},{10... | collective-permute-start | bytes 1769480 | tf_op jit(solution)/shard_map/ppermute | solution.py:18
  21.0 1.6 %collective-permute-start.3 = (bf16[96,1408]{1,0:T(8,128)(2,1)}, bf16[96,1408]{1,0:T(8,128)(2,1)}, u32[]{:S(2)}, u32[]{:S(2)}) collective-permute-start(bf16[96,1408]{1,0:T(8,128)(2,1)} %slice.189), channel_id=1, source_target_pairs={{0,2},{1,3},{2,0},{3,1},{4,6},{5,7},{6,4},{7,5},{8,10},{9,11},{10,... | collective-permute-start | bytes 811016 | tf_op jit(solution)/shard_map/ppermute | solution.py:22
  24.6 2.5 %shard_map.119 = bf16[384,3584]{1,0:T(8,128)(2,1)S(1)} custom-call(s32[8]{0:T(128)S(1)} %iota_xor_fusion.order, bf16[384,3584]{1,0:T(8,128)(2,1)S(1)} %bitcast.101, f32[384,28]{1,0:T(8,128)S(1)} %bitcast.105, bf16[384,3584]{1,0:T(8,128)(2,1)S(1)} %bitcast.102, f32[384,28]{1,0:T(8,128)S(1)} %bitcast.106, bf16[384,3584]{1,0:T(8,128)(2,1)S(1)} %bitcast.103, ...), custom_call_target="tpu_custom_call" | custom-call | flops 1376256 | bytes 5505024 | tf_op jit(solution)/shard_map/pallas_call | solution.py:57
  27.1 1.5 %copy-done.1 = bf16[384,3584]{1,0:T(8,128)(2,1)} copy-done((bf16[384,3584]{1,0:T(8,128)(2,1)}, bf16[384,3584]{1,0:T(8,128)(2,1)S(1)}, u32[]{:S(2)}) %copy-start.1) | copy-done | bytes 2752536
  28.7 1.4 collective-permute-done.4
  30.1 4.2 %collective-permute-done.3 = bf16[96,1408]{1,0:T(8,128)(2,1)} collective-permute-done((bf16[96,1408]{1,0:T(8,128)(2,1)}, bf16[96,1408]{1,0:T(8,128)(2,1)}, u32[]{:S(2)}, u32[]{:S(2)}) %collective-permute-start.3) | collective-permute-done | bytes 270368 | tf_op jit(solution)/shard_map/ppermute | solution.py:22
  37.1 2.5 %collective-permute-start.6 = (bf16[96,1408]{1,0:T(8,128)(2,1)S(1)}, bf16[96,1408]{1,0:T(8,128)(2,1)S(1)}, u32[]{:S(2)}, u32[]{:S(2)}) collective-permute-start(bf16[96,1408]{1,0:T(8,128)(2,1)S(1)} %slice.192), channel_id=1, source_target_pairs={{0,2},{1,3},{2,0},{3,1},{4,6},{5,7},{6,4},{7,5},{8,10},{9,11},{10,... | collective-permute-start | bytes 811016 | tf_op jit(solution)/shard_map/ppermute | solution.py:22
  39.6 1.4 convolution_convert_fusion.4
  42.5 5.6 %fusion = f32[384,1024]{1,0:T(8,128)S(1)} fusion(bf16[384,3584]{1,0:T(8,128)(2,1)S(1)} %copy-done.2, bf16[1,3584,1024]{2,1,0:T(8,128)(2,1)} %param.12), kind=kOutput, calls=%fused_computation.3 | convolution fusion | flops 2818572288 | bytes 11665408 | tf_op jit(solution)/shard_map/dot_general | solution.py:30
  48.1 3.1 %fusion.2 = f32[384,1024]{1,0:T(8,128)S(1)} fusion(bf16[384,3584]{1,0:T(8,128)(2,1)S(1)} %copy-done.2, bf16[1,3584,1024]{2,1,0:T(8,128)(2,1)S(1)} %bitcast.123), kind=kOutput, calls=%fused_computation.5 | convolution fusion | flops 2818572288 | bytes 11665408 | tf_op jit(solution)/shard_map/dot_general | solution.py:30
  51.3 5.4 %collective-permute-done.6 = bf16[96,1408]{1,0:T(8,128)(2,1)S(1)} collective-permute-done((bf16[96,1408]{1,0:T(8,128)(2,1)S(1)}, bf16[96,1408]{1,0:T(8,128)(2,1)S(1)}, u32[]{:S(2)}, u32[]{:S(2)}) %collective-permute-start.6) | collective-permute-done | bytes 270368 | tf_op jit(solution)/shard_map/ppermute | solution.py:22
  56.8 10.6 %collective-permute-done.7 = bf16[96,2304]{1,0:T(8,128)(2,1)S(1)} collective-permute-done((bf16[96,2304]{1,0:T(8,128)(2,1)S(1)}, bf16[96,2304]{1,0:T(8,128)(2,1)S(1)}, u32[]{:S(2)}, u32[]{:S(2)}) %collective-permute-start.7) | collective-permute-done | bytes 442400 | tf_op jit(solution)/shard_map/ppermute | solution.py:22
  75.9 4.5 %collective-permute-done.10 = bf16[48,2304]{1,0:T(8,128)(2,1)S(1)} collective-permute-done((bf16[48,2304]{1,0:T(8,128)(2,1)S(1)}, bf16[48,2304]{1,0:T(8,128)(2,1)S(1)}, u32[]{:S(2)}, u32[]{:S(2)}) %collective-permute-start.10) | collective-permute-done | bytes 221216 | tf_op jit(solution)/shard_map/ppermute | solution.py:22
  80.6 2.0 %fusion.7 = f32[384,1024]{1,0:T(8,128)S(1)} fusion(bf16[384,2304]{1,0:T(8,128)(2,1)S(1)} %constant_dynamic-update-slice_fusion.1, bf16[1024,3584]{1,0:T(8,128)(2,1)S(1)} %bitcast.119), kind=kOutput, calls=%fused_computation.11 | convolution fusion | flops 1811939328 | bytes 8060928 | tf_op jit(solution)/shard_map/dot_general | solution.py:30
  88.1 1.7 %collective-permute-start.15 = (bf16[48,1280]{1,0:T(8,128)(2,1)S(1)}, bf16[48,1280]{1,0:T(8,128)(2,1)S(1)}, u32[]{:S(2)}, u32[]{:S(2)}) collective-permute-start(bf16[48,1280]{1,0:T(8,128)(2,1)S(1)} %get-tuple-element.209), channel_id=1, source_target_pairs={{0,2},{1,3},{2,0},{3,1},{4,6},{5,7},{6,4},{7,5},{8,10},{9,11},{10,... | collective-permute-start | bytes 368648 | tf_op jit(solution)/shard_map/ppermute | solution.py:22
  90.0 2.1 %fusion.9 = f32[384,2304]{1,0:T(8,128)S(1)} fusion(bf16[384,1024]{1,0:T(8,128)(2,1)S(1)} %get-tuple-element.191, bf16[1,3584,1024]{2,1,0:T(8,128)(2,1)S(1)} %bitcast.121), kind=kOutput, calls=%fused_computation.13 | convolution fusion | flops 1811939328 | bytes 9043968 | tf_op jit(solution)/shard_map/dot_general | solution.py:30
  92.1 2.3 %fusion.18 = bf16[384,2304]{1,0:T(8,128)(2,1)S(1)} fusion(f32[384,2304]{1,0:T(8,128)S(1)} %fusion.9, bf16[384,1024]{1,0:T(8,128)(2,1)S(1)} %multiply_convert_fusion.1, bf16[1,3584,1024]{2,1,0:T(8,128)(2,1)S(1)} %bitcast.123), kind=kOutput, calls=%fused_computation.20 | convolution fusion | flops 1813708800 | bytes 10813440 | tf_op jit(solution)/shard_map/dot_general | solution.py:30
  96.5 1.4 collective-permute-start.18
  99.1 1.8 %collective-permute-start.21 = (bf16[48,3712]{1,0:T(8,128)(2,1)S(1)}, bf16[48,3712]{1,0:T(8,128)(2,1)S(1)}, u32[]{:S(2)}, u32[]{:S(2)}) collective-permute-start(bf16[48,3712]{1,0:T(8,128)(2,1)S(1)} %slice.240), channel_id=1, source_target_pairs={{0,2},{1,3},{2,0},{3,1},{4,6},{5,7},{6,4},{7,5},{8,10},{9,11},{10,... | collective-permute-start | bytes 1069064 | tf_op jit(solution)/shard_map/ppermute | solution.py:22
  100.9 6.1 %convolution_convert_fusion.2 = bf16[3584,1024]{1,0:T(8,128)(2,1)} fusion(bf16[384,3584]{1,0:T(8,128)(2,1)S(1)} %copy-done.2, bf16[384,1024]{1,0:T(8,128)(2,1)S(1)} %multiply_convert_fusion.1), kind=kOutput, calls=%fused_computation.2 | convolution fusion | flops 2822242304 | bytes 10878976 | tf_op jit(solution)/shard_map/dot_general | solution.py:30
  107.0 4.2 %collective-permute-done.19 = bf16[48,2432]{1,0:T(8,128)(2,1)S(1)} collective-permute-done((bf16[48,2432]{1,0:T(8,128)(2,1)S(1)}, bf16[48,2432]{1,0:T(8,128)(2,1)S(1)}, u32[]{:S(2)}, u32[]{:S(2)}) %collective-permute-start.19) | collective-permute-done | bytes 233504 | tf_op jit(solution)/shard_map/ppermute | solution.py:22
  111.2 5.3 %collective-permute-done.18 = bf16[48,2432]{1,0:T(8,128)(2,1)S(1)} collective-permute-done((bf16[48,2432]{1,0:T(8,128)(2,1)S(1)}, bf16[48,2432]{1,0:T(8,128)(2,1)S(1)}, u32[]{:S(2)}, u32[]{:S(2)}) %collective-permute-start.18) | collective-permute-done | bytes 233504 | tf_op jit(solution)/shard_map/ppermute | solution.py:22
  117.3 2.0 %collective-permute-start.24 = (bf16[128,2432]{1,0:T(8,128)(2,1)S(1)}, bf16[128,2432]{1,0:T(8,128)(2,1)S(1)}, u32[]{:S(2)}, u32[]{:S(2)}) collective-permute-start(bf16[128,2432]{1,0:T(8,128)(2,1)S(1)} %convolution_convert_fusion.5), channel_id=1, source_target_pairs={{0,4},{1,5},{2,6},{3,7},{4,0},{5,1},{6,2},{7,3},{8,12},{9,13},{10,... | collective-permute-start | bytes 1867784 | tf_op jit(solution)/shard_map/ppermute | solution.py:22
  119.3 6.1 %fusion.4 = bf16[1,3584,1024]{2,1,0:T(8,128)(2,1)} fusion(bf16[384,3584]{1,0:T(8,128)(2,1)S(1)} %copy-done.2, bf16[384,1024]{1,0:T(8,128)(2,1)S(1)} %get-tuple-element.191), kind=kOutput, calls=%fused_computation.7 | convolution fusion | flops 2822242304 | bytes 10878976 | tf_op jit(solution)/shard_map/dot_general | solution.py:30
  125.4 6.2 %fusion.5 = bf16[1,1024,3584]{2,1,0:T(8,128)(2,1)} fusion(bf16[384,1024]{1,0:T(8,128)(2,1)S(1)} %get-tuple-element.192, bf16[384,2304]{1,0:T(8,128)(2,1)S(1)} %constant_dynamic-update-slice_fusion.1, bf16[384,1280]{1,0:T(8,128)(2,1)S(1)} %slice.248), kind=kOutput, calls=%fused_computation.8 | convolution fusion | flops 2827747328 | bytes 10878976 | tf_op jit(solution)/shard_map/dot_general | solution.py:30
  131.6 2.8 %collective-permute-done.21 = bf16[48,3712]{1,0:T(8,128)(2,1)S(1)} collective-permute-done((bf16[48,3712]{1,0:T(8,128)(2,1)S(1)}, bf16[48,3712]{1,0:T(8,128)(2,1)S(1)}, u32[]{:S(2)}, u32[]{:S(2)}) %collective-permute-start.21) | collective-permute-done | bytes 356384 | tf_op jit(solution)/shard_map/ppermute | solution.py:22
  134.4 7.6 %collective-permute-done.22 = bf16[48,3712]{1,0:T(8,128)(2,1)S(1)} collective-permute-done((bf16[48,3712]{1,0:T(8,128)(2,1)S(1)}, bf16[48,3712]{1,0:T(8,128)(2,1)S(1)}, u32[]{:S(2)}, u32[]{:S(2)}) %collective-permute-start.22) | collective-permute-done | bytes 356384 | tf_op jit(solution)/shard_map/ppermute | solution.py:22
  142.1 5.8 %collective-permute-done.24 = bf16[128,2432]{1,0:T(8,128)(2,1)S(1)} collective-permute-done((bf16[128,2432]{1,0:T(8,128)(2,1)S(1)}, bf16[128,2432]{1,0:T(8,128)(2,1)S(1)}, u32[]{:S(2)}, u32[]{:S(2)}) %collective-permute-start.24) | collective-permute-done | bytes 622624 | tf_op jit(solution)/shard_map/ppermute | solution.py:22
  (158 shorter events, 30.8 us)
Async XLA Ops:
  0.6 7.0 %copy-start.7 = (s32[1,128,2]{1,2,0:T(2,128)S(1)}, s32[1,128,2]{1,2,0:T(2,128)}, u32[]{:S(2)}) copy-start(s32[1,128,2]{1,2,0:T(2,128)} %param.9) | copy-start | bytes 3076
  0.6 7.2 %copy-start.6 = (f32[1,384,28]{1,0,2:T(1,128)S(1)}, f32[1,384,28]{1,0,2:T(1,128)}, u32[]{:S(2)}) copy-start(f32[1,384,28]{1,0,2:T(1,128)} %param.15) | copy-start | bytes 129028
  0.7 8.1 %copy-start.13 = (f32[1,128,2]{1,2,0:T(2,128)S(1)}, f32[1,128,2]{1,2,0:T(2,128)}, u32[]{:S(2)}) copy-start(f32[1,128,2]{1,2,0:T(2,128)} %param.10) | copy-start | bytes 3076
  1.7 10.9 %collective-permute-start = (bf16[128,1280]{1,0:T(8,128)(2,1)S(1)}, bf16[128,1280]{1,0:T(8,128)(2,1)}, u32[]{:S(2)}, u32[]{:S(2)}) collective-permute-start(bf16[128,1280]{1,0:T(8,128)(2,1)S(1)} %slice_bitcast_fusion.2), channel_id=1, source_target_pairs={{0,24},{8,0},{16,8},{24,16},{1,25},{9,1},{17,9},{25,17},{2,26},{10... | collective-permute-start | bytes 983048 | tf_op jit(solution)/shard_map/ppermute | solution.py:18
  7.5 17.1 %copy-start = (bf16[1,384,3584]{2,1,0:T(8,128)(2,1)S(1)}, bf16[1,384,3584]{2,1,0:T(8,128)(2,1)}, u32[]{:S(2)}) copy-start(bf16[1,384,3584]{2,1,0:T(8,128)(2,1)} %param.14) | copy-start | bytes 8257540
  12.6 21.6 %collective-permute-start.1 = (bf16[128,1280]{1,0:T(8,128)(2,1)}, bf16[128,1280]{1,0:T(8,128)(2,1)}, u32[]{:S(2)}, u32[]{:S(2)}) collective-permute-start(bf16[128,1280]{1,0:T(8,128)(2,1)} %collective-permute-done), channel_id=1, source_target_pairs={{0,4},{1,5},{2,6},{3,7},{4,0},{5,1},{6,2},{7,3},{8,12},{9,13},{10,... | collective-permute-start | bytes 983048 | tf_op jit(solution)/shard_map/ppermute | solution.py:22
  16.7 17.6 %collective-permute-start.2 = (bf16[128,2304]{1,0:T(8,128)(2,1)}, bf16[128,2304]{1,0:T(8,128)(2,1)}, u32[]{:S(2)}, u32[]{:S(2)}) collective-permute-start(bf16[128,2304]{1,0:T(8,128)(2,1)} %slice_bitcast_fusion.1), channel_id=1, source_target_pairs={{0,24},{8,0},{16,8},{24,16},{1,25},{9,1},{17,9},{25,17},{2,26},{10... | collective-permute-start | bytes 1769480 | tf_op jit(solution)/shard_map/ppermute | solution.py:18
  21.0 13.2 %collective-permute-start.3 = (bf16[96,1408]{1,0:T(8,128)(2,1)}, bf16[96,1408]{1,0:T(8,128)(2,1)}, u32[]{:S(2)}, u32[]{:S(2)}) collective-permute-start(bf16[96,1408]{1,0:T(8,128)(2,1)} %slice.189), channel_id=1, source_target_pairs={{0,2},{1,3},{2,0},{3,1},{4,6},{5,7},{6,4},{7,5},{8,10},{9,11},{10,... | collective-permute-start | bytes 811016 | tf_op jit(solution)/shard_map/ppermute | solution.py:22
  23.8 6.3 %collective-permute-start.4 = (f32[2,8,128]{2,1,0:T(8,128)S(1)}, f32[2,8,128]{2,1,0:T(8,128)S(1)}, u32[]{:S(2)}, u32[]{:S(2)}) collective-permute-start(f32[2,8,128]{2,1,0:T(8,128)S(1)} %pad_maximum_fusion.8), channel_id=1, source_target_pairs={{0,4},{1,5},{2,6},{3,7},{4,0},{5,1},{6,2},{7,3},{8,12},{9,13},{10,... | collective-permute-start | bytes 24584 | tf_op jit(solution)/shard_map/ppermute | solution.py:22
  36.5 30.9 %collective-permute-start.5 = (bf16[128,2304]{1,0:T(8,128)(2,1)}, bf16[128,2304]{1,0:T(8,128)(2,1)S(1)}, u32[]{:S(2)}, u32[]{:S(2)}) collective-permute-start(bf16[128,2304]{1,0:T(8,128)(2,1)} %collective-permute-done.2), channel_id=1, source_target_pairs={{0,4},{1,5},{2,6},{3,7},{4,0},{5,1},{6,2},{7,3},{8,12},{9,13},{10,... | collective-permute-start | bytes 1769480 | tf_op jit(solution)/shard_map/ppermute | solution.py:22
  37.1 19.7 %collective-permute-start.6 = (bf16[96,1408]{1,0:T(8,128)(2,1)S(1)}, bf16[96,1408]{1,0:T(8,128)(2,1)S(1)}, u32[]{:S(2)}, u32[]{:S(2)}) collective-permute-start(bf16[96,1408]{1,0:T(8,128)(2,1)S(1)} %slice.192), channel_id=1, source_target_pairs={{0,2},{1,3},{2,0},{3,1},{4,6},{5,7},{6,4},{7,5},{8,10},{9,11},{10,... | collective-permute-start | bytes 811016 | tf_op jit(solution)/shard_map/ppermute | solution.py:22
  42.1 9.2 %collective-permute-start.8 = (bf16[96,1408]{1,0:T(8,128)(2,1)S(1)}, bf16[96,1408]{1,0:T(8,128)(2,1)S(1)}, u32[]{:S(2)}, u32[]{:S(2)}) collective-permute-start(bf16[96,1408]{1,0:T(8,128)(2,1)S(1)} %pad_maximum_fusion.6), channel_id=1, source_target_pairs={{0,1},{1,0},{2,3},{3,2},{4,5},{5,4},{6,7},{7,6},{8,9},{9,8},{10,11... | collective-permute-start | bytes 811016 | tf_op jit(solution)/shard_map/ppermute | solution.py:22
  42.2 5.9 %slice-start.6 = ((s8[7340032]{0:T(1024)(128)(4,1)}), s8[4194304]{0:T(1024)(128)(4,1)S(1)}, s32[]{:S(2)}) async-start(s8[7340032]{0:T(1024)(128)(4,1)} %bitcast.122), calls=%async_computation.6 | async-start | bytes 8388608
  42.2 5.8 %slice-start.7 = ((s8[7340032]{0:T(1024)(128)(4,1)}), s8[3145728]{0:T(1024)(128)(4,1)S(1)}, s32[]{:S(2)}) async-start(s8[7340032]{0:T(1024)(128)(4,1)} %bitcast.122), calls=%async_computation.7 | async-start | bytes 6291456
  42.2 25.2 %collective-permute-start.7 = (bf16[96,2304]{1,0:T(8,128)(2,1)S(1)}, bf16[96,2304]{1,0:T(8,128)(2,1)S(1)}, u32[]{:S(2)}, u32[]{:S(2)}) collective-permute-start(bf16[96,2304]{1,0:T(8,128)(2,1)S(1)} %slice.193), channel_id=1, source_target_pairs={{0,2},{1,3},{2,0},{3,1},{4,6},{5,7},{6,4},{7,5},{8,10},{9,11},{10,... | collective-permute-start | bytes 1327112 | tf_op jit(solution)/shard_map/ppermute | solution.py:22
  68.2 7.7 %collective-permute-start.11 = (bf16[48,2304]{1,0:T(8,128)(2,1)S(1)}, bf16[48,2304]{1,0:T(8,128)(2,1)S(1)}, u32[]{:S(2)}, u32[]{:S(2)}) collective-permute-start(bf16[48,2304]{1,0:T(8,128)(2,1)S(1)} %get-tuple-element.214), channel_id=1, source_target_pairs={{0,3},{1,2},{2,1},{3,0},{4,7},{5,6},{6,5},{7,4},{8,11},{9,10},{10,... | collective-permute-start | bytes 663560 | tf_op jit(solution)/shard_map/ppermute | solution.py:22
  68.2 12.2 %collective-permute-start.10 = (bf16[48,2304]{1,0:T(8,128)(2,1)S(1)}, bf16[48,2304]{1,0:T(8,128)(2,1)S(1)}, u32[]{:S(2)}, u32[]{:S(2)}) collective-permute-start(bf16[48,2304]{1,0:T(8,128)(2,1)S(1)} %get-tuple-element.215), channel_id=1, source_target_pairs={{0,2},{1,3},{2,0},{3,1},{4,6},{5,7},{6,4},{7,5},{8,10},{9,11},{10,... | collective-permute-start | bytes 663560 | tf_op jit(solution)/shard_map/ppermute | solution.py:22
  69.5 10.9 %collective-permute-start.9 = (bf16[48,2304]{1,0:T(8,128)(2,1)S(1)}, bf16[48,2304]{1,0:T(8,128)(2,1)S(1)}, u32[]{:S(2)}, u32[]{:S(2)}) collective-permute-start(bf16[48,2304]{1,0:T(8,128)(2,1)S(1)} %get-tuple-element.216), channel_id=1, source_target_pairs={{0,1},{1,0},{2,3},{3,2},{4,5},{5,4},{6,7},{7,6},{8,9},{9,8},{10,11... | collective-permute-start | bytes 663560 | tf_op jit(solution)/shard_map/ppermute | solution.py:22
  70.2 1.6 %collective-permute-start.13 = (bf16[96,1408]{1,0:T(8,128)(2,1)S(1)}, bf16[96,1408]{1,0:T(8,128)(2,1)S(1)}, u32[]{:S(2)}, u32[]{:S(2)}) collective-permute-start(bf16[96,1408]{1,0:T(8,128)(2,1)S(1)} %pad_maximum_fusion.7), channel_id=1, source_target_pairs={{0,1},{1,0},{2,3},{3,2},{4,5},{5,4},{6,7},{7,6},{8,9},{9,8},{10,11... | collective-permute-start | bytes 811016 | tf_op jit(solution)/shard_map/ppermute | solution.py:22
  70.4 10.0 %collective-permute-start.12 = (bf16[96,2304]{1,0:T(8,128)(2,1)S(1)}, bf16[96,2304]{1,0:T(8,128)(2,1)S(1)}, u32[]{:S(2)}, u32[]{:S(2)}) collective-permute-start(bf16[96,2304]{1,0:T(8,128)(2,1)S(1)} %pad_maximum_fusion.5), channel_id=1, source_target_pairs={{0,1},{1,0},{2,3},{3,2},{4,5},{5,4},{6,7},{7,6},{8,9},{9,8},{10,11... | collective-permute-start | bytes 1327112 | tf_op jit(solution)/shard_map/ppermute | solution.py:22
  74.0 6.4 %copy-start.5 = (bf16[96,2304]{1,0:T(8,128)(2,1)S(1)}, bf16[96,2304]{1,0:T(8,128)(2,1)}, u32[]{:S(2)}) copy-start(bf16[96,2304]{1,0:T(8,128)(2,1)} %copy-done.4) | copy-start | bytes 1327108
  88.1 7.6 %collective-permute-start.16 = (bf16[48,1280]{1,0:T(8,128)(2,1)S(1)}, bf16[48,1280]{1,0:T(8,128)(2,1)S(1)}, u32[]{:S(2)}, u32[]{:S(2)}) collective-permute-start(bf16[48,1280]{1,0:T(8,128)(2,1)S(1)} %get-tuple-element.208), channel_id=1, source_target_pairs={{0,3},{1,2},{2,1},{3,0},{4,7},{5,6},{6,5},{7,4},{8,11},{9,10},{10,... | collective-permute-start | bytes 368648 | tf_op jit(solution)/shard_map/ppermute | solution.py:22
  88.1 8.3 %collective-permute-start.15 = (bf16[48,1280]{1,0:T(8,128)(2,1)S(1)}, bf16[48,1280]{1,0:T(8,128)(2,1)S(1)}, u32[]{:S(2)}, u32[]{:S(2)}) collective-permute-start(bf16[48,1280]{1,0:T(8,128)(2,1)S(1)} %get-tuple-element.209), channel_id=1, source_target_pairs={{0,2},{1,3},{2,0},{3,1},{4,6},{5,7},{6,4},{7,5},{8,10},{9,11},{10,... | collective-permute-start | bytes 368648 | tf_op jit(solution)/shard_map/ppermute | solution.py:22
  89.9 6.5 %collective-permute-start.14 = (bf16[48,1280]{1,0:T(8,128)(2,1)S(1)}, bf16[48,1280]{1,0:T(8,128)(2,1)S(1)}, u32[]{:S(2)}, u32[]{:S(2)}) collective-permute-start(bf16[48,1280]{1,0:T(8,128)(2,1)S(1)} %get-tuple-element.210), channel_id=1, source_target_pairs={{0,1},{1,0},{2,3},{3,2},{4,5},{5,4},{6,7},{7,6},{8,9},{9,8},{10,11... | collective-permute-start | bytes 368648 | tf_op jit(solution)/shard_map/ppermute | solution.py:22
  96.5 14.8 %collective-permute-start.19 = (bf16[48,2432]{1,0:T(8,128)(2,1)S(1)}, bf16[48,2432]{1,0:T(8,128)(2,1)S(1)}, u32[]{:S(2)}, u32[]{:S(2)}) collective-permute-start(bf16[48,2432]{1,0:T(8,128)(2,1)S(1)} %get-tuple-element.200), channel_id=1, source_target_pairs={{0,3},{1,2},{2,1},{3,0},{4,7},{5,6},{6,5},{7,4},{8,11},{9,10},{10,... | collective-permute-start | bytes 700424 | tf_op jit(solution)/shard_map/ppermute | solution.py:22
  96.5 20.0 %collective-permute-start.18 = (bf16[48,2432]{1,0:T(8,128)(2,1)S(1)}, bf16[48,2432]{1,0:T(8,128)(2,1)S(1)}, u32[]{:S(2)}, u32[]{:S(2)}) collective-permute-start(bf16[48,2432]{1,0:T(8,128)(2,1)S(1)} %get-tuple-element.201), channel_id=1, source_target_pairs={{0,2},{1,3},{2,0},{3,1},{4,6},{5,7},{6,4},{7,5},{8,10},{9,11},{10,... | collective-permute-start | bytes 700424 | tf_op jit(solution)/shard_map/ppermute | solution.py:22
  98.0 18.6 %collective-permute-start.17 = (bf16[48,2432]{1,0:T(8,128)(2,1)S(1)}, bf16[48,2432]{1,0:T(8,128)(2,1)S(1)}, u32[]{:S(2)}, u32[]{:S(2)}) collective-permute-start(bf16[48,2432]{1,0:T(8,128)(2,1)S(1)} %get-tuple-element.202), channel_id=1, source_target_pairs={{0,1},{1,0},{2,3},{3,2},{4,5},{5,4},{6,7},{7,6},{8,9},{9,8},{10,11... | collective-permute-start | bytes 700424 | tf_op jit(solution)/shard_map/ppermute | solution.py:22
  98.7 32.9 %collective-permute-start.23 = (bf16[128,1280]{1,0:T(8,128)(2,1)S(1)}, bf16[128,1280]{1,0:T(8,128)(2,1)S(1)}, u32[]{:S(2)}, u32[]{:S(2)}) collective-permute-start(bf16[128,1280]{1,0:T(8,128)(2,1)S(1)} %convolution_convert_fusion.8), channel_id=1, source_target_pairs={{0,4},{1,5},{2,6},{3,7},{4,0},{5,1},{6,2},{7,3},{8,12},{9,13},{10,... | collective-permute-start | bytes 983048 | tf_op jit(solution)/shard_map/ppermute | solution.py:22
  99.1 35.3 %collective-permute-start.21 = (bf16[48,3712]{1,0:T(8,128)(2,1)S(1)}, bf16[48,3712]{1,0:T(8,128)(2,1)S(1)}, u32[]{:S(2)}, u32[]{:S(2)}) collective-permute-start(bf16[48,3712]{1,0:T(8,128)(2,1)S(1)} %slice.240), channel_id=1, source_target_pairs={{0,2},{1,3},{2,0},{3,1},{4,6},{5,7},{6,4},{7,5},{8,10},{9,11},{10,... | collective-permute-start | bytes 1069064 | tf_op jit(solution)/shard_map/ppermute | solution.py:22
  117.0 25.0 %collective-permute-start.22 = (bf16[48,3712]{1,0:T(8,128)(2,1)S(1)}, bf16[48,3712]{1,0:T(8,128)(2,1)S(1)}, u32[]{:S(2)}, u32[]{:S(2)}) collective-permute-start(bf16[48,3712]{1,0:T(8,128)(2,1)S(1)} %get-tuple-element.206), channel_id=1, source_target_pairs={{0,3},{1,2},{2,1},{3,0},{4,7},{5,6},{6,5},{7,4},{8,11},{9,10},{10,... | collective-permute-start | bytes 1069064 | tf_op jit(solution)/shard_map/ppermute | solution.py:22
  117.1 25.0 %collective-permute-start.20 = (bf16[48,3712]{1,0:T(8,128)(2,1)S(1)}, bf16[48,3712]{1,0:T(8,128)(2,1)S(1)}, u32[]{:S(2)}, u32[]{:S(2)}) collective-permute-start(bf16[48,3712]{1,0:T(8,128)(2,1)S(1)} %get-tuple-element.207), channel_id=1, source_target_pairs={{0,1},{1,0},{2,3},{3,2},{4,5},{5,4},{6,7},{7,6},{8,9},{9,8},{10,11... | collective-permute-start | bytes 1069064 | tf_op jit(solution)/shard_map/ppermute | solution.py:22
  117.3 30.6 %collective-permute-start.24 = (bf16[128,2432]{1,0:T(8,128)(2,1)S(1)}, bf16[128,2432]{1,0:T(8,128)(2,1)S(1)}, u32[]{:S(2)}, u32[]{:S(2)}) collective-permute-start(bf16[128,2432]{1,0:T(8,128)(2,1)S(1)} %convolution_convert_fusion.5), channel_id=1, source_target_pairs={{0,4},{1,5},{2,6},{3,7},{4,0},{5,1},{6,2},{7,3},{8,12},{9,13},{10,... | collective-permute-start | bytes 1867784 | tf_op jit(solution)/shard_map/ppermute | solution.py:22
  (16 other events, 33.7 us)
where the time goes:
time: 151 us; the launch traced here: 150 us
  waiting for transfers between devices  58 us (38%)
  matrix products  43.1 us (29%)
  starting transfers between devices  26.1 us (17%)
  local copies, waits for them, and re-layouts  11.7 us (8%)
  other arithmetic  7.29 us (5%)
  Pallas kernels  2.48 us (2%)
    ppermute x23, waiting for transfers between devices, swap(): return lax.ppermute(x, EXPERT, [(i, i ^ bit) for i in range(8)])  54.2 us
    dot_general x21, matrix products, mm(): lax.dot_general(a, b, (dims, ((), ())), preferred_element_type=jnp.float32)  43.1 us
    ppermute x23, starting transfers between devices, swap(): return lax.ppermute(x, EXPERT, [(i, i ^ bit) for i in range(8)])  18.8 us
    ppermute x2, starting transfers between devices, shifted(): return lax.ppermute(x, axis, [(i, (i + by) % size) for i in range(size)])  7.34 us
    unnamed x53, local copies, waits for them, and re-layouts  4.78 us
    ppermute x2, waiting for transfers between devices, shifted(): return lax.ppermute(x, axis, [(i, (i + by) % size) for i in range(size)])  3.81 us
  transfers between devices with their start and end apart: 25, of which 14 were waited for; matrix products, arithmetic and copies ran while one was open for 30% of the time, Pallas kernels for 2%

commit v1 on v0

--- a/solution.py
+++ b/solution.py
@@ -9,7 +9,7 @@
 SECTION = "section"
 EXPERTS = 8
 CAP = 48
-OUT_CUTS = (10, 18)
+OUT_CUTS = (7, 21)
 BACK_CUTS = (10, 18)
 
 
@@ -65,7 +65,7 @@
         out_shape=jax.ShapeDtypeStruct((count, width), jnp.bfloat16),
         compiler_params=pltpu.CompilerParams(vmem_limit_bytes=24 * 2**20),
         cost_estimate=pl.CostEstimate(
-            flops=count * width, bytes_accessed=4 * count * width, transcendentals=0
+            flops=1, bytes_accessed=1, transcendentals=0
         ),
     )(order, *[codes, scales] * at_once)
 
@@ -86,6 +86,7 @@
     codes, scales = stash_q[0], stash_scale[0]
     pieces = [upstream[0, :, lo:hi] for lo, hi in spans]
     xs = [shifted(pieces[0], SECTION, -1)]
+    x1 = shifted(pieces[1], SECTION, -1)
 
     route = routes[0].T
     ids = jnp.arange(EXPERTS, dtype=jnp.int32)
@@ -126,18 +127,19 @@
     )
 
     cross = swap(x, 4)
-    x1 = shifted(pieces[1], SECTION, -1)
     own = jnp.concatenate([pack(near_sel, x), pack(near_sel, gate_columns(both[1, :4]))], axis=1)
     own, both, codes = together(own, both, codes)
     near_own = swap(own[2 * CAP :], 2)
     far_both = swap(both, 4)
     inputs = scaled_blocks(me ^ jnp.arange(8, dtype=jnp.int32), codes, scales)
-    cross, x, own, near_own, far_both, inputs = together(cross, x1, own, near_own, far_both, inputs)
+    far_sel = selection(far_both[0, 4:])
+    gates_far = pack(far_sel, gate_columns(far_both[1, 4:]))
+    cross, x, own, near_own, far_sel, gates_far, inputs = together(
+        cross, x1, own, near_own, far_sel, gates_far, inputs
+    )
 
     next_cross = swap(x, 4)
-    far_sel = selection(far_both[0, 4:])
-    far = [pack(far_sel, cross), pack(far_sel, gate_columns(far_both[1, 4:]))]
-    far = jnp.concatenate(far, axis=1)
+    far = jnp.concatenate([pack(far_sel, cross), gates_far], axis=1)
     far, x, own, near_own, inputs = together(far, x, own, near_own, inputs)
     near_far = swap(far[2 * CAP :], 2)
     own_1 = pack(near_sel, x)

time: 151 us -> 148 us (0.980)
  starting transfers between devices: 26.1 us -> 22.9 us
  waiting for transfers between devices: 58 us -> 60.6 us
  other arithmetic: 7.29 us -> 4.97 us
    ppermute x23, waiting for transfers between devices: 54.2 us -> 59.3 us  [swap(): return lax.ppermute(x, EXPERT, [(i, i ^ bit) for i in range(8)])]
    ppermute x2, starting transfers between devices: 7.34 us -> 4.48 us  [shifted(): return lax.ppermute(x, axis, [(i, (i + by) % size) for i in range(size)])]
    ppermute x2, waiting for transfers between devices: 3.81 us -> 1.32 us  [shifted(): return lax.ppermute(x, axis, [(i, (i + by) % size) for i in range(size)])]
    unnamed x53 -> x35, local copies, waits for them, and re-layouts: 4.78 us -> 5.34 us
  transfers between devices with their start and end apart: 25 -> 25, of which waited for: 14 -> 14; matrix products, arithmetic and copies ran while one was open for 30% -> 31% of each run, Pallas kernels for 2% -> 2%
where the time goes in v1:
time: 148 us
  waiting for transfers between devices  60.6 us (41%)
  matrix products  43.1 us (29%)
  starting transfers between devices  22.9 us (15%)
  local copies, waits for them, and re-layouts  12.4 us (8%)
  other arithmetic  4.97 us (3%)
  Pallas kernels  2.48 us (2%)
    ppermute x23, waiting for transfers between devices, swap(): return lax.ppermute(x, EXPERT, [(i, i ^ bit) for i in range(8)])  59.3 us
    dot_general x21, matrix products, mm(): lax.dot_general(a, b, (dims, ((), ())), preferred_element_type=jnp.float32)  43.1 us
    ppermute x23, starting transfers between devices, swap(): return lax.ppermute(x, EXPERT, [(i, i ^ bit) for i in range(8)])  18.4 us
    unnamed x35, local copies, waits for them, and re-layouts  5.34 us
    ppermute x2, starting transfers between devices, shifted(): return lax.ppermute(x, axis, [(i, (i + by) % size) for i in range(size)])  4.48 us
    squeeze x2, local copies, waits for them, and re-layouts, relayed(): pieces = [upstream[0, :, lo:hi] for lo, hi in spans]  3.1 us
  transfers between devices with their start and end apart: 25, of which 14 were waited for; matrix products, arithmetic and copies ran while one was open for 31% of the time, Pallas kernels for 2%

profile of v1, /device:TPU:0, one launch (start us, length us, event | category | flops | bytes accessed | tf_op | source)
XLA Modules:
  0.0 147.8 jit_solution(16172359450883610394)
XLA Ops:
  1.8 3.9 %collective-permute-start = (bf16[128,896]{1,0:T(8,128)(2,1)S(1)}, bf16[128,896]{1,0:T(8,128)(2,1)}, u32[]{:S(2)}, u32[]{:S(2)}) collective-permute-start(bf16[128,896]{1,0:T(8,128)(2,1)S(1)} %slice_bitcast_fusion.2), channel_id=1, source_target_pairs={{0,24},{8,0},{16,8},{24,16},{1,25},{9,1},{17,9},{25,17},{2,26},{10... | collective-permute-start | bytes 688136 | tf_op jit(solution)/shard_map/ppermute | solution.py:18
  5.7 2.0 %slice_bitcast_fusion.1 = bf16[128,2688]{1,0:T(8,128)(2,1)} fusion(bf16[1,128,3584]{2,1,0:T(8,128)(2,1)} %param.8), kind=kLoop, calls=%fused_computation.70 | loop fusion | bytes 1376256 | tf_op jit(solution)/shard_map/squeeze | solution.py:87
  10.4 1.3 collective-permute-done
  13.2 2.7 %collective-permute-start.4 = (f32[2,8,128]{2,1,0:T(8,128)S(1)}, f32[2,8,128]{2,1,0:T(8,128)S(1)}, u32[]{:S(2)}, u32[]{:S(2)}) collective-permute-start(f32[2,8,128]{2,1,0:T(8,128)S(1)} %pad_maximum_fusion.8), channel_id=1, source_target_pairs={{0,4},{1,5},{2,6},{3,7},{4,0},{5,1},{6,2},{7,3},{8,12},{9,13},{10,... | collective-permute-start | bytes 24584 | tf_op jit(solution)/shard_map/ppermute | solution.py:22
  16.8 1.6 %collective-permute-start.3 = (bf16[96,1024]{1,0:T(8,128)(2,1)}, bf16[96,1024]{1,0:T(8,128)(2,1)}, u32[]{:S(2)}, u32[]{:S(2)}) collective-permute-start(bf16[96,1024]{1,0:T(8,128)(2,1)} %slice.189), channel_id=1, source_target_pairs={{0,2},{1,3},{2,0},{3,1},{4,6},{5,7},{6,4},{7,5},{8,10},{9,11},{10,... | collective-permute-start | bytes 589832 | tf_op jit(solution)/shard_map/ppermute | solution.py:22
  18.4 2.5 %shard_map.119 = bf16[384,3584]{1,0:T(8,128)(2,1)S(1)} custom-call(s32[8]{0:T(128)S(1)} %iota_xor_fusion.order, bf16[384,3584]{1,0:T(8,128)(2,1)S(1)} %bitcast.106, f32[384,28]{1,0:T(8,128)S(1)} %bitcast.110, bf16[384,3584]{1,0:T(8,128)(2,1)S(1)} %bitcast.107, f32[384,28]{1,0:T(8,128)S(1)} %bitcast.111, bf16[384,3584]{1,0:T(8,128)(2,1)S(1)} %bitcast.108, ...), custom_call_target="tpu_custom_call" | custom-call | flops 1 | bytes 1 | tf_op jit(solution)/shard_map/pallas_call | solution.py:57
  20.9 1.5 %copy-done.1 = bf16[384,3584]{1,0:T(8,128)(2,1)} copy-done((bf16[384,3584]{1,0:T(8,128)(2,1)}, bf16[384,3584]{1,0:T(8,128)(2,1)S(1)}, u32[]{:S(2)}) %copy-start.1) | copy-done | bytes 2752536
  22.8 2.2 %collective-permute-done.3 = bf16[96,1024]{1,0:T(8,128)(2,1)} collective-permute-done((bf16[96,1024]{1,0:T(8,128)(2,1)}, bf16[96,1024]{1,0:T(8,128)(2,1)}, u32[]{:S(2)}, u32[]{:S(2)}) %collective-permute-start.3) | collective-permute-done | bytes 196640 | tf_op jit(solution)/shard_map/ppermute | solution.py:22
  25.0 2.4 %collective-permute-done.1 = bf16[128,896]{1,0:T(8,128)(2,1)} collective-permute-done((bf16[128,896]{1,0:T(8,128)(2,1)}, bf16[128,896]{1,0:T(8,128)(2,1)}, u32[]{:S(2)}, u32[]{:S(2)}) %collective-permute-start.1) | collective-permute-done | bytes 229408 | tf_op jit(solution)/shard_map/ppermute | solution.py:22
  29.5 2.3 %collective-permute-start.6 = (bf16[96,1024]{1,0:T(8,128)(2,1)S(1)}, bf16[96,1024]{1,0:T(8,128)(2,1)S(1)}, u32[]{:S(2)}, u32[]{:S(2)}) collective-permute-start(bf16[96,1024]{1,0:T(8,128)(2,1)S(1)} %slice.192), channel_id=1, source_target_pairs={{0,2},{1,3},{2,0},{3,1},{4,6},{5,7},{6,4},{7,5},{8,10},{9,11},{10,... | collective-permute-start | bytes 589832 | tf_op jit(solution)/shard_map/ppermute | solution.py:22
  31.8 1.5 %convolution_convert_fusion.4 = bf16[192,2688]{1,0:T(8,128)(2,1)S(1)} fusion(bf16[192,128]{1,0:T(8,128)(2,1)S(1)} %fusion.56, bf16[128,2688]{1,0:T(8,128)(2,1)} %collective-permute-done.2), kind=kOutput, calls=%fused_computation.22 | convolution fusion | flops 132636672 | bytes 1769472 | tf_op jit(solution)/shard_map/dot_general | solution.py:30
  34.7 5.6 %fusion = f32[384,1024]{1,0:T(8,128)S(1)} fusion(bf16[384,3584]{1,0:T(8,128)(2,1)S(1)} %copy-done.2, bf16[1,3584,1024]{2,1,0:T(8,128)(2,1)} %param.12), kind=kOutput, calls=%fused_computation.3 | convolution fusion | flops 2818572288 | bytes 11665408 | tf_op jit(solution)/shard_map/dot_general | solution.py:30
  40.3 3.1 %fusion.2 = f32[384,1024]{1,0:T(8,128)S(1)} fusion(bf16[384,3584]{1,0:T(8,128)(2,1)S(1)} %copy-done.2, bf16[1,3584,1024]{2,1,0:T(8,128)(2,1)S(1)} %bitcast.128), kind=kOutput, calls=%fused_computation.5 | convolution fusion | flops 2818572288 | bytes 11665408 | tf_op jit(solution)/shard_map/dot_general | solution.py:30
  43.5 5.0 %collective-permute-done.6 = bf16[96,1024]{1,0:T(8,128)(2,1)S(1)} collective-permute-done((bf16[96,1024]{1,0:T(8,128)(2,1)S(1)}, bf16[96,1024]{1,0:T(8,128)(2,1)S(1)}, u32[]{:S(2)}, u32[]{:S(2)}) %collective-permute-start.6) | collective-permute-done | bytes 196640 | tf_op jit(solution)/shard_map/ppermute | solution.py:22
  48.5 14.8 %collective-permute-done.7 = bf16[96,2688]{1,0:T(8,128)(2,1)S(1)} collective-permute-done((bf16[96,2688]{1,0:T(8,128)(2,1)S(1)}, bf16[96,2688]{1,0:T(8,128)(2,1)S(1)}, u32[]{:S(2)}, u32[]{:S(2)}) %collective-permute-start.7) | collective-permute-done | bytes 516128 | tf_op jit(solution)/shard_map/ppermute | solution.py:22
  70.6 1.8 %collective-permute-done.11 = bf16[48,2688]{1,0:T(8,128)(2,1)S(1)} collective-permute-done((bf16[48,2688]{1,0:T(8,128)(2,1)S(1)}, bf16[48,2688]{1,0:T(8,128)(2,1)S(1)}, u32[]{:S(2)}, u32[]{:S(2)}) %collective-permute-start.11) | collective-permute-done | bytes 258080 | tf_op jit(solution)/shard_map/ppermute | solution.py:22
  72.4 5.3 %collective-permute-done.10 = bf16[48,2688]{1,0:T(8,128)(2,1)S(1)} collective-permute-done((bf16[48,2688]{1,0:T(8,128)(2,1)S(1)}, bf16[48,2688]{1,0:T(8,128)(2,1)S(1)}, u32[]{:S(2)}, u32[]{:S(2)}) %collective-permute-start.10) | collective-permute-done | bytes 258080 | tf_op jit(solution)/shard_map/ppermute | solution.py:22
  77.9 2.4 %fusion.6 = f32[384,1024]{1,0:T(8,128)S(1)} fusion(bf16[384,2688]{1,0:T(8,128)(2,1)S(1)} %constant_dynamic-update-slice_fusion.1, bf16[1024,3584]{1,0:T(8,128)(2,1)S(1)} %bitcast.124), kind=kOutput, calls=%fused_computation.9 | convolution fusion | flops 2113929216 | bytes 9142272 | tf_op jit(solution)/shard_map/dot_general | solution.py:30
  85.9 1.7 %collective-permute-start.15 = (bf16[48,1280]{1,0:T(8,128)(2,1)S(1)}, bf16[48,1280]{1,0:T(8,128)(2,1)S(1)}, u32[]{:S(2)}, u32[]{:S(2)}) collective-permute-start(bf16[48,1280]{1,0:T(8,128)(2,1)S(1)} %get-tuple-element.214), channel_id=1, source_target_pairs={{0,2},{1,3},{2,0},{3,1},{4,6},{5,7},{6,4},{7,5},{8,10},{9,11},{10,... | collective-permute-start | bytes 368648 | tf_op jit(solution)/shard_map/ppermute | solution.py:22
  87.8 2.0 %fusion.9 = f32[384,2304]{1,0:T(8,128)S(1)} fusion(bf16[384,1024]{1,0:T(8,128)(2,1)S(1)} %get-tuple-element.191, bf16[1,3584,1024]{2,1,0:T(8,128)(2,1)S(1)} %bitcast.126), kind=kOutput, calls=%fused_computation.13 | convolution fusion | flops 1811939328 | bytes 9043968 | tf_op jit(solution)/shard_map/dot_general | solution.py:30
  89.8 2.3 %fusion.18 = bf16[384,2304]{1,0:T(8,128)(2,1)S(1)} fusion(f32[384,2304]{1,0:T(8,128)S(1)} %fusion.9, bf16[384,1024]{1,0:T(8,128)(2,1)S(1)} %multiply_convert_fusion.1, bf16[1,3584,1024]{2,1,0:T(8,128)(2,1)S(1)} %bitcast.128), kind=kOutput, calls=%fused_computation.20 | convolution fusion | flops 1813708800 | bytes 10813440 | tf_op jit(solution)/shard_map/dot_general | solution.py:30
  94.3 1.4 collective-permute-start.18
  96.6 1.8 %collective-permute-start.21 = (bf16[48,3712]{1,0:T(8,128)(2,1)S(1)}, bf16[48,3712]{1,0:T(8,128)(2,1)S(1)}, u32[]{:S(2)}, u32[]{:S(2)}) collective-permute-start(bf16[48,3712]{1,0:T(8,128)(2,1)S(1)} %slice.240), channel_id=1, source_target_pairs={{0,2},{1,3},{2,0},{3,1},{4,6},{5,7},{6,4},{7,5},{8,10},{9,11},{10,... | collective-permute-start | bytes 1069064 | tf_op jit(solution)/shard_map/ppermute | solution.py:22
  98.4 6.1 %convolution_convert_fusion.2 = bf16[3584,1024]{1,0:T(8,128)(2,1)} fusion(bf16[384,3584]{1,0:T(8,128)(2,1)S(1)} %copy-done.2, bf16[384,1024]{1,0:T(8,128)(2,1)S(1)} %multiply_convert_fusion.1), kind=kOutput, calls=%fused_computation.2 | convolution fusion | flops 2822242304 | bytes 10878976 | tf_op jit(solution)/shard_map/dot_general | solution.py:30
  104.5 4.3 %collective-permute-done.19 = bf16[48,2432]{1,0:T(8,128)(2,1)S(1)} collective-permute-done((bf16[48,2432]{1,0:T(8,128)(2,1)S(1)}, bf16[48,2432]{1,0:T(8,128)(2,1)S(1)}, u32[]{:S(2)}, u32[]{:S(2)}) %collective-permute-start.19) | collective-permute-done | bytes 233504 | tf_op jit(solution)/shard_map/ppermute | solution.py:22
  108.8 5.5 %collective-permute-done.18 = bf16[48,2432]{1,0:T(8,128)(2,1)S(1)} collective-permute-done((bf16[48,2432]{1,0:T(8,128)(2,1)S(1)}, bf16[48,2432]{1,0:T(8,128)(2,1)S(1)}, u32[]{:S(2)}, u32[]{:S(2)}) %collective-permute-start.18) | collective-permute-done | bytes 233504 | tf_op jit(solution)/shard_map/ppermute | solution.py:22
  115.0 1.8 %collective-permute-start.24 = (bf16[128,2432]{1,0:T(8,128)(2,1)S(1)}, bf16[128,2432]{1,0:T(8,128)(2,1)S(1)}, u32[]{:S(2)}, u32[]{:S(2)}) collective-permute-start(bf16[128,2432]{1,0:T(8,128)(2,1)S(1)} %convolution_convert_fusion.5), channel_id=1, source_target_pairs={{0,4},{1,5},{2,6},{3,7},{4,0},{5,1},{6,2},{7,3},{8,12},{9,13},{10,... | collective-permute-start | bytes 1867784 | tf_op jit(solution)/shard_map/ppermute | solution.py:22
  116.8 6.1 %fusion.4 = bf16[1,3584,1024]{2,1,0:T(8,128)(2,1)} fusion(bf16[384,3584]{1,0:T(8,128)(2,1)S(1)} %copy-done.2, bf16[384,1024]{1,0:T(8,128)(2,1)S(1)} %get-tuple-element.191), kind=kOutput, calls=%fused_computation.7 | convolution fusion | flops 2822242304 | bytes 10878976 | tf_op jit(solution)/shard_map/dot_general | solution.py:30
  122.8 6.2 %fusion.5 = bf16[1,1024,3584]{2,1,0:T(8,128)(2,1)} fusion(bf16[384,1024]{1,0:T(8,128)(2,1)S(1)} %get-tuple-element.192, bf16[384,2688]{1,0:T(8,128)(2,1)S(1)} %constant_dynamic-update-slice_fusion.1, bf16[384,896]{1,0:T(8,128)(2,1)S(1)} %slice.250), kind=kOutput, calls=%fused_computation.8 | convolution fusion | flops 2827747328 | bytes 10878976 | tf_op jit(solution)/shard_map/dot_general | solution.py:30
  129.0 2.9 %collective-permute-done.21 = bf16[48,3712]{1,0:T(8,128)(2,1)S(1)} collective-permute-done((bf16[48,3712]{1,0:T(8,128)(2,1)S(1)}, bf16[48,3712]{1,0:T(8,128)(2,1)S(1)}, u32[]{:S(2)}, u32[]{:S(2)}) %collective-permute-start.21) | collective-permute-done | bytes 356384 | tf_op jit(solution)/shard_map/ppermute | solution.py:22
  132.0 7.6 %collective-permute-done.22 = bf16[48,3712]{1,0:T(8,128)(2,1)S(1)} collective-permute-done((bf16[48,3712]{1,0:T(8,128)(2,1)S(1)}, bf16[48,3712]{1,0:T(8,128)(2,1)S(1)}, u32[]{:S(2)}, u32[]{:S(2)}) %collective-permute-start.22) | collective-permute-done | bytes 356384 | tf_op jit(solution)/shard_map/ppermute | solution.py:22
  139.6 6.0 %collective-permute-done.24 = bf16[128,2432]{1,0:T(8,128)(2,1)S(1)} collective-permute-done((bf16[128,2432]{1,0:T(8,128)(2,1)S(1)}, bf16[128,2432]{1,0:T(8,128)(2,1)S(1)}, u32[]{:S(2)}, u32[]{:S(2)}) %collective-permute-start.24) | collective-permute-done | bytes 622624 | tf_op jit(solution)/shard_map/ppermute | solution.py:22
  (139 shorter events, 28.8 us)
Async XLA Ops:
  0.6 9.7 %copy-start.4 = (s32[1,128,2]{1,2,0:T(2,128)S(1)}, s32[1,128,2]{1,2,0:T(2,128)}, u32[]{:S(2)}) copy-start(s32[1,128,2]{1,2,0:T(2,128)} %param.9) | copy-start | bytes 3076
  0.6 9.7 %copy-start.5 = (f32[1,128,2]{1,2,0:T(2,128)S(1)}, f32[1,128,2]{1,2,0:T(2,128)}, u32[]{:S(2)}) copy-start(f32[1,128,2]{1,2,0:T(2,128)} %param.10) | copy-start | bytes 3076
  0.7 17.8 %copy-start = (bf16[1,384,3584]{2,1,0:T(8,128)(2,1)S(1)}, bf16[1,384,3584]{2,1,0:T(8,128)(2,1)}, u32[]{:S(2)}) copy-start(bf16[1,384,3584]{2,1,0:T(8,128)(2,1)} %param.14) | copy-start | bytes 8257540
  1.8 10.0 %collective-permute-start = (bf16[128,896]{1,0:T(8,128)(2,1)S(1)}, bf16[128,896]{1,0:T(8,128)(2,1)}, u32[]{:S(2)}, u32[]{:S(2)}) collective-permute-start(bf16[128,896]{1,0:T(8,128)(2,1)S(1)} %slice_bitcast_fusion.2), channel_id=1, source_target_pairs={{0,24},{8,0},{16,8},{24,16},{1,25},{9,1},{17,9},{25,17},{2,26},{10... | collective-permute-start | bytes 688136 | tf_op jit(solution)/shard_map/ppermute | solution.py:18
  7.7 19.7 %collective-permute-start.2 = (bf16[128,2688]{1,0:T(8,128)(2,1)}, bf16[128,2688]{1,0:T(8,128)(2,1)}, u32[]{:S(2)}, u32[]{:S(2)}) collective-permute-start(bf16[128,2688]{1,0:T(8,128)(2,1)} %slice_bitcast_fusion.1), channel_id=1, source_target_pairs={{0,24},{8,0},{16,8},{24,16},{1,25},{9,1},{17,9},{25,17},{2,26},{10... | collective-permute-start | bytes 2064392 | tf_op jit(solution)/shard_map/ppermute | solution.py:18
  13.2 9.3 %collective-permute-start.4 = (f32[2,8,128]{2,1,0:T(8,128)S(1)}, f32[2,8,128]{2,1,0:T(8,128)S(1)}, u32[]{:S(2)}, u32[]{:S(2)}) collective-permute-start(f32[2,8,128]{2,1,0:T(8,128)S(1)} %pad_maximum_fusion.8), channel_id=1, source_target_pairs={{0,4},{1,5},{2,6},{3,7},{4,0},{5,1},{6,2},{7,3},{8,12},{9,13},{10,... | collective-permute-start | bytes 24584 | tf_op jit(solution)/shard_map/ppermute | solution.py:22
  15.8 11.5 %collective-permute-start.1 = (bf16[128,896]{1,0:T(8,128)(2,1)}, bf16[128,896]{1,0:T(8,128)(2,1)}, u32[]{:S(2)}, u32[]{:S(2)}) collective-permute-start(bf16[128,896]{1,0:T(8,128)(2,1)} %collective-permute-done), channel_id=1, source_target_pairs={{0,4},{1,5},{2,6},{3,7},{4,0},{5,1},{6,2},{7,3},{8,12},{9,13},{10,... | collective-permute-start | bytes 688136 | tf_op jit(solution)/shard_map/ppermute | solution.py:22
  16.8 8.1 %collective-permute-start.3 = (bf16[96,1024]{1,0:T(8,128)(2,1)}, bf16[96,1024]{1,0:T(8,128)(2,1)}, u32[]{:S(2)}, u32[]{:S(2)}) collective-permute-start(bf16[96,1024]{1,0:T(8,128)(2,1)} %slice.189), channel_id=1, source_target_pairs={{0,2},{1,3},{2,0},{3,1},{4,6},{5,7},{6,4},{7,5},{8,10},{9,11},{10,... | collective-permute-start | bytes 589832 | tf_op jit(solution)/shard_map/ppermute | solution.py:22
  27.4 35.9 %collective-permute-start.5 = (bf16[128,2688]{1,0:T(8,128)(2,1)}, bf16[128,2688]{1,0:T(8,128)(2,1)S(1)}, u32[]{:S(2)}, u32[]{:S(2)}) collective-permute-start(bf16[128,2688]{1,0:T(8,128)(2,1)} %collective-permute-done.2), channel_id=1, source_target_pairs={{0,4},{1,5},{2,6},{3,7},{4,0},{5,1},{6,2},{7,3},{8,12},{9,13},{10,... | collective-permute-start | bytes 2064392 | tf_op jit(solution)/shard_map/ppermute | solution.py:22
  29.5 5.2 %copy-start.2 = (bf16[384,3584]{1,0:T(8,128)(2,1)S(1)}, bf16[384,3584]{1,0:T(8,128)(2,1)}, u32[]{:S(2)}) copy-start(bf16[384,3584]{1,0:T(8,128)(2,1)} %copy-done.1) | copy-start | bytes 8257540
  29.5 19.1 %collective-permute-start.6 = (bf16[96,1024]{1,0:T(8,128)(2,1)S(1)}, bf16[96,1024]{1,0:T(8,128)(2,1)S(1)}, u32[]{:S(2)}, u32[]{:S(2)}) collective-permute-start(bf16[96,1024]{1,0:T(8,128)(2,1)S(1)} %slice.192), channel_id=1, source_target_pairs={{0,2},{1,3},{2,0},{3,1},{4,6},{5,7},{6,4},{7,5},{8,10},{9,11},{10,... | collective-permute-start | bytes 589832 | tf_op jit(solution)/shard_map/ppermute | solution.py:22
  34.3 9.2 %collective-permute-start.8 = (bf16[96,1024]{1,0:T(8,128)(2,1)S(1)}, bf16[96,1024]{1,0:T(8,128)(2,1)S(1)}, u32[]{:S(2)}, u32[]{:S(2)}) collective-permute-start(bf16[96,1024]{1,0:T(8,128)(2,1)S(1)} %pad_maximum_fusion.6), channel_id=1, source_target_pairs={{0,1},{1,0},{2,3},{3,2},{4,5},{5,4},{6,7},{7,6},{8,9},{9,8},{10,11... | collective-permute-start | bytes 589832 | tf_op jit(solution)/shard_map/ppermute | solution.py:22
  34.4 5.9 %slice-start.5 = ((s8[7340032]{0:T(1024)(128)(4,1)}), s8[4194304]{0:T(1024)(128)(4,1)S(1)}, s32[]{:S(2)}) async-start(s8[7340032]{0:T(1024)(128)(4,1)} %bitcast.127), calls=%async_computation.5 | async-start | bytes 8388608
  34.4 5.9 %slice-start.6 = ((s8[7340032]{0:T(1024)(128)(4,1)}), s8[3145728]{0:T(1024)(128)(4,1)S(1)}, s32[]{:S(2)}) async-start(s8[7340032]{0:T(1024)(128)(4,1)} %bitcast.127), calls=%async_computation.6 | async-start | bytes 6291456
  34.5 28.8 %collective-permute-start.7 = (bf16[96,2688]{1,0:T(8,128)(2,1)S(1)}, bf16[96,2688]{1,0:T(8,128)(2,1)S(1)}, u32[]{:S(2)}, u32[]{:S(2)}) collective-permute-start(bf16[96,2688]{1,0:T(8,128)(2,1)S(1)} %slice.193), channel_id=1, source_target_pairs={{0,2},{1,3},{2,0},{3,1},{4,6},{5,7},{6,4},{7,5},{8,10},{9,11},{10,... | collective-permute-start | bytes 1548296 | tf_op jit(solution)/shard_map/ppermute | solution.py:22
  63.8 8.6 %collective-permute-start.11 = (bf16[48,2688]{1,0:T(8,128)(2,1)S(1)}, bf16[48,2688]{1,0:T(8,128)(2,1)S(1)}, u32[]{:S(2)}, u32[]{:S(2)}) collective-permute-start(bf16[48,2688]{1,0:T(8,128)(2,1)S(1)} %get-tuple-element.210), channel_id=1, source_target_pairs={{0,3},{1,2},{2,1},{3,0},{4,7},{5,6},{6,5},{7,4},{8,11},{9,10},{10,... | collective-permute-start | bytes 774152 | tf_op jit(solution)/shard_map/ppermute | solution.py:22
  63.9 13.8 %collective-permute-start.10 = (bf16[48,2688]{1,0:T(8,128)(2,1)S(1)}, bf16[48,2688]{1,0:T(8,128)(2,1)S(1)}, u32[]{:S(2)}, u32[]{:S(2)}) collective-permute-start(bf16[48,2688]{1,0:T(8,128)(2,1)S(1)} %get-tuple-element.211), channel_id=1, source_target_pairs={{0,2},{1,3},{2,0},{3,1},{4,6},{5,7},{6,4},{7,5},{8,10},{9,11},{10,... | collective-permute-start | bytes 774152 | tf_op jit(solution)/shard_map/ppermute | solution.py:22
  65.2 12.5 %collective-permute-start.9 = (bf16[48,2688]{1,0:T(8,128)(2,1)S(1)}, bf16[48,2688]{1,0:T(8,128)(2,1)S(1)}, u32[]{:S(2)}, u32[]{:S(2)}) collective-permute-start(bf16[48,2688]{1,0:T(8,128)(2,1)S(1)} %get-tuple-element.212), channel_id=1, source_target_pairs={{0,1},{1,0},{2,3},{3,2},{4,5},{5,4},{6,7},{7,6},{8,9},{9,8},{10,11... | collective-permute-start | bytes 774152 | tf_op jit(solution)/shard_map/ppermute | solution.py:22
  65.8 3.0 %slice-start.1 = ((s8[7340032]{0:T(1024)(128)(4,1)}), s8[4194304]{0:T(1024)(128)(4,1)S(1)}, s32[]{:S(2)}) async-start(s8[7340032]{0:T(1024)(128)(4,1)} %bitcast.121), calls=%async_computation.1 | async-start | bytes 8388608
  65.8 1.5 %collective-permute-start.13 = (bf16[96,1024]{1,0:T(8,128)(2,1)S(1)}, bf16[96,1024]{1,0:T(8,128)(2,1)S(1)}, u32[]{:S(2)}, u32[]{:S(2)}) collective-permute-start(bf16[96,1024]{1,0:T(8,128)(2,1)S(1)} %pad_maximum_fusion.7), channel_id=1, source_target_pairs={{0,1},{1,0},{2,3},{3,2},{4,5},{5,4},{6,7},{7,6},{8,9},{9,8},{10,11... | collective-permute-start | bytes 589832 | tf_op jit(solution)/shard_map/ppermute | solution.py:22
  66.0 11.7 %collective-permute-start.12 = (bf16[96,2688]{1,0:T(8,128)(2,1)S(1)}, bf16[96,2688]{1,0:T(8,128)(2,1)S(1)}, u32[]{:S(2)}, u32[]{:S(2)}) collective-permute-start(bf16[96,2688]{1,0:T(8,128)(2,1)S(1)} %pad_maximum_fusion.2), channel_id=1, source_target_pairs={{0,1},{1,0},{2,3},{3,2},{4,5},{5,4},{6,7},{7,6},{8,9},{9,8},{10,11... | collective-permute-start | bytes 1548296 | tf_op jit(solution)/shard_map/ppermute | solution.py:22
  85.9 7.5 %collective-permute-start.16 = (bf16[48,1280]{1,0:T(8,128)(2,1)S(1)}, bf16[48,1280]{1,0:T(8,128)(2,1)S(1)}, u32[]{:S(2)}, u32[]{:S(2)}) collective-permute-start(bf16[48,1280]{1,0:T(8,128)(2,1)S(1)} %get-tuple-element.213), channel_id=1, source_target_pairs={{0,3},{1,2},{2,1},{3,0},{4,7},{5,6},{6,5},{7,4},{8,11},{9,10},{10,... | collective-permute-start | bytes 368648 | tf_op jit(solution)/shard_map/ppermute | solution.py:22
  85.9 8.3 %collective-permute-start.15 = (bf16[48,1280]{1,0:T(8,128)(2,1)S(1)}, bf16[48,1280]{1,0:T(8,128)(2,1)S(1)}, u32[]{:S(2)}, u32[]{:S(2)}) collective-permute-start(bf16[48,1280]{1,0:T(8,128)(2,1)S(1)} %get-tuple-element.214), channel_id=1, source_target_pairs={{0,2},{1,3},{2,0},{3,1},{4,6},{5,7},{6,4},{7,5},{8,10},{9,11},{10,... | collective-permute-start | bytes 368648 | tf_op jit(solution)/shard_map/ppermute | solution.py:22
  87.6 6.5 %collective-permute-start.14 = (bf16[48,1280]{1,0:T(8,128)(2,1)S(1)}, bf16[48,1280]{1,0:T(8,128)(2,1)S(1)}, u32[]{:S(2)}, u32[]{:S(2)}) collective-permute-start(bf16[48,1280]{1,0:T(8,128)(2,1)S(1)} %get-tuple-element.215), channel_id=1, source_target_pairs={{0,1},{1,0},{2,3},{3,2},{4,5},{5,4},{6,7},{7,6},{8,9},{9,8},{10,11... | collective-permute-start | bytes 368648 | tf_op jit(solution)/shard_map/ppermute | solution.py:22
  94.2 14.6 %collective-permute-start.19 = (bf16[48,2432]{1,0:T(8,128)(2,1)S(1)}, bf16[48,2432]{1,0:T(8,128)(2,1)S(1)}, u32[]{:S(2)}, u32[]{:S(2)}) collective-permute-start(bf16[48,2432]{1,0:T(8,128)(2,1)S(1)} %get-tuple-element.200), channel_id=1, source_target_pairs={{0,3},{1,2},{2,1},{3,0},{4,7},{5,6},{6,5},{7,4},{8,11},{9,10},{10,... | collective-permute-start | bytes 700424 | tf_op jit(solution)/shard_map/ppermute | solution.py:22
  94.3 20.0 %collective-permute-start.18 = (bf16[48,2432]{1,0:T(8,128)(2,1)S(1)}, bf16[48,2432]{1,0:T(8,128)(2,1)S(1)}, u32[]{:S(2)}, u32[]{:S(2)}) collective-permute-start(bf16[48,2432]{1,0:T(8,128)(2,1)S(1)} %get-tuple-element.201), channel_id=1, source_target_pairs={{0,2},{1,3},{2,0},{3,1},{4,6},{5,7},{6,4},{7,5},{8,10},{9,11},{10,... | collective-permute-start | bytes 700424 | tf_op jit(solution)/shard_map/ppermute | solution.py:22
  95.7 18.6 %collective-permute-start.17 = (bf16[48,2432]{1,0:T(8,128)(2,1)S(1)}, bf16[48,2432]{1,0:T(8,128)(2,1)S(1)}, u32[]{:S(2)}, u32[]{:S(2)}) collective-permute-start(bf16[48,2432]{1,0:T(8,128)(2,1)S(1)} %get-tuple-element.202), channel_id=1, source_target_pairs={{0,1},{1,0},{2,3},{3,2},{4,5},{5,4},{6,7},{7,6},{8,9},{9,8},{10,11... | collective-permute-start | bytes 700424 | tf_op jit(solution)/shard_map/ppermute | solution.py:22
  96.4 32.7 %collective-permute-start.23 = (bf16[128,1280]{1,0:T(8,128)(2,1)S(1)}, bf16[128,1280]{1,0:T(8,128)(2,1)S(1)}, u32[]{:S(2)}, u32[]{:S(2)}) collective-permute-start(bf16[128,1280]{1,0:T(8,128)(2,1)S(1)} %convolution_convert_fusion.6), channel_id=1, source_target_pairs={{0,4},{1,5},{2,6},{3,7},{4,0},{5,1},{6,2},{7,3},{8,12},{9,13},{10,... | collective-permute-start | bytes 983048 | tf_op jit(solution)/shard_map/ppermute | solution.py:22
  96.6 35.4 %collective-permute-start.21 = (bf16[48,3712]{1,0:T(8,128)(2,1)S(1)}, bf16[48,3712]{1,0:T(8,128)(2,1)S(1)}, u32[]{:S(2)}, u32[]{:S(2)}) collective-permute-start(bf16[48,3712]{1,0:T(8,128)(2,1)S(1)} %slice.240), channel_id=1, source_target_pairs={{0,2},{1,3},{2,0},{3,1},{4,6},{5,7},{6,4},{7,5},{8,10},{9,11},{10,... | collective-permute-start | bytes 1069064 | tf_op jit(solution)/shard_map/ppermute | solution.py:22
  114.7 24.9 %collective-permute-start.22 = (bf16[48,3712]{1,0:T(8,128)(2,1)S(1)}, bf16[48,3712]{1,0:T(8,128)(2,1)S(1)}, u32[]{:S(2)}, u32[]{:S(2)}) collective-permute-start(bf16[48,3712]{1,0:T(8,128)(2,1)S(1)} %get-tuple-element.206), channel_id=1, source_target_pairs={{0,3},{1,2},{2,1},{3,0},{4,7},{5,6},{6,5},{7,4},{8,11},{9,10},{10,... | collective-permute-start | bytes 1069064 | tf_op jit(solution)/shard_map/ppermute | solution.py:22
  114.8 24.8 %collective-permute-start.20 = (bf16[48,3712]{1,0:T(8,128)(2,1)S(1)}, bf16[48,3712]{1,0:T(8,128)(2,1)S(1)}, u32[]{:S(2)}, u32[]{:S(2)}) collective-permute-start(bf16[48,3712]{1,0:T(8,128)(2,1)S(1)} %get-tuple-element.207), channel_id=1, source_target_pairs={{0,1},{1,0},{2,3},{3,2},{4,5},{5,4},{6,7},{7,6},{8,9},{9,8},{10,11... | collective-permute-start | bytes 1069064 | tf_op jit(solution)/shard_map/ppermute | solution.py:22
  115.0 30.6 %collective-permute-start.24 = (bf16[128,2432]{1,0:T(8,128)(2,1)S(1)}, bf16[128,2432]{1,0:T(8,128)(2,1)S(1)}, u32[]{:S(2)}, u32[]{:S(2)}) collective-permute-start(bf16[128,2432]{1,0:T(8,128)(2,1)S(1)} %convolution_convert_fusion.5), channel_id=1, source_target_pairs={{0,4},{1,5},{2,6},{3,7},{4,0},{5,1},{6,2},{7,3},{8,12},{9,13},{10,... | collective-permute-start | bytes 1867784 | tf_op jit(solution)/shard_map/ppermute | solution.py:22
  (6 other events, 10.4 us)

commit v2 on v1

--- a/solution.py
+++ b/solution.py
@@ -10,7 +10,7 @@
 EXPERTS = 8
 CAP = 48
 OUT_CUTS = (7, 21)
-BACK_CUTS = (10, 18)
+BACK_CUTS = (14, 14)
 
 
 def shifted(x, axis, by):
@@ -212,7 +212,9 @@
     back[1] = back_of(1, *rest[:2])
     back[1] = jnp.concatenate([back[1], gate_terms(rest[4], rest[3])], axis=1)
     near_back = jnp.concatenate([back[j][:half] for j in range(steps)], axis=1)
-    hands, back, rest, near_back = together(hands, back, rest, near_back)
+    given = swap(stacked(near_back[CAP : 2 * CAP], near_back[3 * CAP :]), 1)
+    hands, back, rest, near_back, given = together(hands, back, rest, near_back, given)
+    near_sent = stacked(near_back[2 * CAP : 3 * CAP], given[CAP:])
 
     def crossing(name, hands):
         far_sum = mm(far_sel, stacked(*hands), ((0,), (0,))).astype(bf16)
@@ -222,16 +224,15 @@
     far_sum = crossing(0, hands)
     far_sum, rest, near_back = together(far_sum, rest, near_back)
     crossed = [swap(far_sum, 4)]
-    near = traded("rnear", near_back, (2,))
+    near = swap(near_sent, 2)
     grad_gw = mm(rest[2], rest[0], ((0,), (0,))).astype(bf16)
     hands, grad_gw, rest, near_back = together(more, grad_gw, rest, near_back)
     far_sum = crossing(1, hands)
     far_sum, rest, near_back = together(far_sum, rest, near_back)
     crossed.append(swap(far_sum, 4))
-    near.update(traded("rnear", near_back, (3, 1)))
     grad_uw = mm(rest[2], rest[1], ((0,), (0,))).astype(bf16)
     grad_dw = mm(rest[5], jnp.concatenate(rest[6], axis=1), ((0,), (0,))).astype(bf16)
-    total = mm(near_sel, stacked(near_back[:CAP], near[1], near[2], near[3]), ((0,), (0,)))
+    total = mm(near_sel, stacked(near_back[:CAP], given[:CAP], near), ((0,), (0,)))
     total = (total + jnp.concatenate(crossed, axis=1).astype(f32)).astype(bf16)
     terms, grad_input = total[:, width:].astype(f32), total[:, :width]
     wanted = column[None] // 3 == routes[0][:, :, None]

time: 148 us -> 145 us (0.980)
  local copies, waits for them, and re-layouts: 12.4 us -> 10.9 us
    ppermute x23 -> x22, starting transfers between devices: 18.4 us -> 17.1 us  [swap(): return lax.ppermute(x, EXPERT, [(i, i ^ bit) for i in range(8)])]
    unnamed x35 -> x39, local copies, waits for them, and re-layouts: 5.34 us -> 4.12 us
    ppermute x23 -> x22, waiting for transfers between devices: 59.3 us -> 59.3 us  [swap(): return lax.ppermute(x, EXPERT, [(i, i ^ bit) for i in range(8)])]
  transfers between devices with their start and end apart: 25 -> 24, of which waited for: 14 -> 12; matrix products, arithmetic and copies ran while one was open for 31% -> 31% of each run, Pallas kernels for 2% -> 2%
where the time goes in v2:
time: 145 us
  waiting for transfers between devices  60.6 us (42%)
  matrix products  42.9 us (30%)
  starting transfers between devices  21.6 us (15%)
  local copies, waits for them, and re-layouts  10.9 us (8%)
  other arithmetic  5.13 us (4%)
  Pallas kernels  2.48 us (2%)
    ppermute x22, waiting for transfers between devices, swap(): return lax.ppermute(x, EXPERT, [(i, i ^ bit) for i in range(8)])  59.3 us
    dot_general x21, matrix products, mm(): lax.dot_general(a, b, (dims, ((), ())), preferred_element_type=jnp.float32)  42.9 us
    ppermute x22, starting transfers between devices, swap(): return lax.ppermute(x, EXPERT, [(i, i ^ bit) for i in range(8)])  17.1 us
    ppermute x2, starting transfers between devices, shifted(): return lax.ppermute(x, axis, [(i, (i + by) % size) for i in range(size)])  4.48 us
    unnamed x39, local copies, waits for them, and re-layouts  4.12 us
    squeeze x2, local copies, waits for them, and re-layouts, relayed(): pieces = [upstream[0, :, lo:hi] for lo, hi in spans]  3.1 us
  transfers between devices with their start and end apart: 24, of which 12 were waited for; matrix products, arithmetic and copies ran while one was open for 31% of the time, Pallas kernels for 2%

profile of v2, /device:TPU:0, one launch (start us, length us, event | category | flops | bytes accessed | tf_op | source)
XLA Modules:
  0.0 145.0 jit_solution(7438319443923960668)
XLA Ops:
  1.8 3.9 %collective-permute-start = (bf16[128,896]{1,0:T(8,128)(2,1)S(1)}, bf16[128,896]{1,0:T(8,128)(2,1)}, u32[]{:S(2)}, u32[]{:S(2)}) collective-permute-start(bf16[128,896]{1,0:T(8,128)(2,1)S(1)} %slice_bitcast_fusion.2), channel_id=1, source_target_pairs={{0,24},{8,0},{16,8},{24,16},{1,25},{9,1},{17,9},{25,17},{2,26},{10... | collective-permute-start | bytes 688136 | tf_op jit(solution)/shard_map/ppermute | solution.py:18
  5.7 2.0 %slice_bitcast_fusion.1 = bf16[128,2688]{1,0:T(8,128)(2,1)} fusion(bf16[1,128,3584]{2,1,0:T(8,128)(2,1)} %param.8), kind=kLoop, calls=%fused_computation.82 | loop fusion | bytes 1376256 | tf_op jit(solution)/shard_map/squeeze | solution.py:87
  10.4 1.3 collective-permute-done
  13.2 2.7 %collective-permute-start.4 = (f32[2,8,128]{2,1,0:T(8,128)S(1)}, f32[2,8,128]{2,1,0:T(8,128)S(1)}, u32[]{:S(2)}, u32[]{:S(2)}) collective-permute-start(f32[2,8,128]{2,1,0:T(8,128)S(1)} %pad_maximum_fusion.10), channel_id=1, source_target_pairs={{0,4},{1,5},{2,6},{3,7},{4,0},{5,1},{6,2},{7,3},{8,12},{9,13},{10,... | collective-permute-start | bytes 24584 | tf_op jit(solution)/shard_map/ppermute | solution.py:22
  16.8 1.6 %collective-permute-start.3 = (bf16[96,1024]{1,0:T(8,128)(2,1)}, bf16[96,1024]{1,0:T(8,128)(2,1)}, u32[]{:S(2)}, u32[]{:S(2)}) collective-permute-start(bf16[96,1024]{1,0:T(8,128)(2,1)} %slice.195), channel_id=1, source_target_pairs={{0,2},{1,3},{2,0},{3,1},{4,6},{5,7},{6,4},{7,5},{8,10},{9,11},{10,... | collective-permute-start | bytes 589832 | tf_op jit(solution)/shard_map/ppermute | solution.py:22
  18.4 2.5 %shard_map.119 = bf16[384,3584]{1,0:T(8,128)(2,1)S(1)} custom-call(s32[8]{0:T(128)S(1)} %iota_xor_fusion.order, bf16[384,3584]{1,0:T(8,128)(2,1)S(1)} %bitcast.110, f32[384,28]{1,0:T(8,128)S(1)} %bitcast.114, bf16[384,3584]{1,0:T(8,128)(2,1)S(1)} %bitcast.111, f32[384,28]{1,0:T(8,128)S(1)} %bitcast.115, bf16[384,3584]{1,0:T(8,128)(2,1)S(1)} %bitcast.112, ...), custom_call_target="tpu_custom_call" | custom-call | flops 1 | bytes 1 | tf_op jit(solution)/shard_map/pallas_call | solution.py:57
  20.9 1.5 %copy-done.1 = bf16[384,3584]{1,0:T(8,128)(2,1)} copy-done((bf16[384,3584]{1,0:T(8,128)(2,1)}, bf16[384,3584]{1,0:T(8,128)(2,1)S(1)}, u32[]{:S(2)}) %copy-start.1) | copy-done | bytes 2752536
  22.8 2.2 %collective-permute-done.3 = bf16[96,1024]{1,0:T(8,128)(2,1)} collective-permute-done((bf16[96,1024]{1,0:T(8,128)(2,1)}, bf16[96,1024]{1,0:T(8,128)(2,1)}, u32[]{:S(2)}, u32[]{:S(2)}) %collective-permute-start.3) | collective-permute-done | bytes 196640 | tf_op jit(solution)/shard_map/ppermute | solution.py:22
  25.0 2.4 %collective-permute-done.1 = bf16[128,896]{1,0:T(8,128)(2,1)} collective-permute-done((bf16[128,896]{1,0:T(8,128)(2,1)}, bf16[128,896]{1,0:T(8,128)(2,1)}, u32[]{:S(2)}, u32[]{:S(2)}) %collective-permute-start.1) | collective-permute-done | bytes 229408 | tf_op jit(solution)/shard_map/ppermute | solution.py:22
  29.5 2.3 %collective-permute-start.6 = (bf16[96,1024]{1,0:T(8,128)(2,1)S(1)}, bf16[96,1024]{1,0:T(8,128)(2,1)S(1)}, u32[]{:S(2)}, u32[]{:S(2)}) collective-permute-start(bf16[96,1024]{1,0:T(8,128)(2,1)S(1)} %slice.198), channel_id=1, source_target_pairs={{0,2},{1,3},{2,0},{3,1},{4,6},{5,7},{6,4},{7,5},{8,10},{9,11},{10,... | collective-permute-start | bytes 589832 | tf_op jit(solution)/shard_map/ppermute | solution.py:22
  31.8 1.5 %convolution_convert_fusion.4 = bf16[192,2688]{1,0:T(8,128)(2,1)S(1)} fusion(bf16[192,128]{1,0:T(8,128)(2,1)S(1)} %fusion.62, bf16[128,2688]{1,0:T(8,128)(2,1)} %collective-permute-done.2), kind=kOutput, calls=%fused_computation.14 | convolution fusion | flops 132636672 | bytes 1769472 | tf_op jit(solution)/shard_map/dot_general | solution.py:30
  34.7 5.6 %fusion = f32[384,1024]{1,0:T(8,128)S(1)} fusion(bf16[384,3584]{1,0:T(8,128)(2,1)S(1)} %copy-done.2, bf16[1,3584,1024]{2,1,0:T(8,128)(2,1)} %param.12), kind=kOutput, calls=%fused_computation.3 | convolution fusion | flops 2818572288 | bytes 11665408 | tf_op jit(solution)/shard_map/dot_general | solution.py:30
  40.3 3.0 %fusion.2 = f32[384,1024]{1,0:T(8,128)S(1)} fusion(bf16[384,3584]{1,0:T(8,128)(2,1)S(1)} %copy-done.2, bf16[1,3584,1024]{2,1,0:T(8,128)(2,1)S(1)} %bitcast.132), kind=kOutput, calls=%fused_computation.5 | convolution fusion | flops 2818572288 | bytes 11665408 | tf_op jit(solution)/shard_map/dot_general | solution.py:30
  43.4 5.1 %collective-permute-done.6 = bf16[96,1024]{1,0:T(8,128)(2,1)S(1)} collective-permute-done((bf16[96,1024]{1,0:T(8,128)(2,1)S(1)}, bf16[96,1024]{1,0:T(8,128)(2,1)S(1)}, u32[]{:S(2)}, u32[]{:S(2)}) %collective-permute-start.6) | collective-permute-done | bytes 196640 | tf_op jit(solution)/shard_map/ppermute | solution.py:22
  48.5 14.8 %collective-permute-done.7 = bf16[96,2688]{1,0:T(8,128)(2,1)S(1)} collective-permute-done((bf16[96,2688]{1,0:T(8,128)(2,1)S(1)}, bf16[96,2688]{1,0:T(8,128)(2,1)S(1)}, u32[]{:S(2)}, u32[]{:S(2)}) %collective-permute-start.7) | collective-permute-done | bytes 516128 | tf_op jit(solution)/shard_map/ppermute | solution.py:22
  63.9 1.3 collective-permute-start.10
  70.6 1.8 %collective-permute-done.11 = bf16[48,2688]{1,0:T(8,128)(2,1)S(1)} collective-permute-done((bf16[48,2688]{1,0:T(8,128)(2,1)S(1)}, bf16[48,2688]{1,0:T(8,128)(2,1)S(1)}, u32[]{:S(2)}, u32[]{:S(2)}) %collective-permute-start.11) | collective-permute-done | bytes 258080 | tf_op jit(solution)/shard_map/ppermute | solution.py:22
  72.4 5.3 %collective-permute-done.10 = bf16[48,2688]{1,0:T(8,128)(2,1)S(1)} collective-permute-done((bf16[48,2688]{1,0:T(8,128)(2,1)S(1)}, bf16[48,2688]{1,0:T(8,128)(2,1)S(1)}, u32[]{:S(2)}, u32[]{:S(2)}) %collective-permute-start.10) | collective-permute-done | bytes 258080 | tf_op jit(solution)/shard_map/ppermute | solution.py:22
  77.9 2.4 %fusion.6 = f32[384,1024]{1,0:T(8,128)S(1)} fusion(bf16[384,2688]{1,0:T(8,128)(2,1)S(1)} %constant_dynamic-update-slice_fusion.1, bf16[1024,3584]{1,0:T(8,128)(2,1)S(1)} %bitcast.128), kind=kOutput, calls=%fused_computation.9 | convolution fusion | flops 2113929216 | bytes 9142272 | tf_op jit(solution)/shard_map/dot_general | solution.py:30
  81.3 1.6 %fusion.13 = f32[384,1792]{1,0:T(8,128)S(1)} fusion(bf16[384,1024]{1,0:T(8,128)(2,1)S(1)} %multiply_convert_fusion, bf16[1,3584,1024]{2,1,0:T(8,128)(2,1)S(1)} %bitcast.130), kind=kOutput, calls=%fused_computation.19 | convolution fusion | flops 1409286144 | bytes 7208960 | tf_op jit(solution)/shard_map/dot_general | solution.py:30
  83.6 1.6 %fusion.30 = bf16[384,1792]{1,0:T(8,128)(2,1)S(1)} fusion(f32[384,1792]{1,0:T(8,128)S(1)} %fusion.13, bf16[384,1024]{1,0:T(8,128)(2,1)S(1)} %get-tuple-element.171, bf16[1,3584,1024]{2,1,0:T(8,128)(2,1)S(1)} %bitcast.134), kind=kOutput, calls=%fused_computation.30 | convolution fusion | flops 1410662400 | bytes 8585216 | tf_op jit(solution)/shard_map/dot_general | solution.py:30
  85.7 1.7 %collective-permute-start.15 = (bf16[48,1792]{1,0:T(8,128)(2,1)S(1)}, bf16[48,1792]{1,0:T(8,128)(2,1)S(1)}, u32[]{:S(2)}, u32[]{:S(2)}) collective-permute-start(bf16[48,1792]{1,0:T(8,128)(2,1)S(1)} %get-tuple-element.210), channel_id=1, source_target_pairs={{0,2},{1,3},{2,0},{3,1},{4,6},{5,7},{6,4},{7,5},{8,10},{9,11},{10,... | collective-permute-start | bytes 516104 | tf_op jit(solution)/shard_map/ppermute | solution.py:22
  87.5 1.6 %fusion.9 = f32[384,1792]{1,0:T(8,128)S(1)} fusion(bf16[384,1024]{1,0:T(8,128)(2,1)S(1)} %multiply_convert_fusion, bf16[1,3584,1024]{2,1,0:T(8,128)(2,1)S(1)} %bitcast.130), kind=kOutput, calls=%fused_computation.15 | convolution fusion | flops 1409286144 | bytes 7208960 | tf_op jit(solution)/shard_map/dot_general | solution.py:30
  89.2 1.9 %fusion.27 = bf16[384,1792]{1,0:T(8,128)(2,1)S(1)} fusion(f32[384,1792]{1,0:T(8,128)S(1)} %fusion.9, bf16[384,1024]{1,0:T(8,128)(2,1)S(1)} %get-tuple-element.171, bf16[1,3584,1024]{2,1,0:T(8,128)(2,1)S(1)} %bitcast.134), kind=kOutput, calls=%fused_computation.29 | convolution fusion | flops 1410662400 | bytes 8585216 | tf_op jit(solution)/shard_map/dot_general | solution.py:30
  92.1 3.9 %collective-permute-done.15 = bf16[48,1792]{1,0:T(8,128)(2,1)S(1)} collective-permute-done((bf16[48,1792]{1,0:T(8,128)(2,1)S(1)}, bf16[48,1792]{1,0:T(8,128)(2,1)S(1)}, u32[]{:S(2)}, u32[]{:S(2)}) %collective-permute-start.15) | collective-permute-done | bytes 172064 | tf_op jit(solution)/shard_map/ppermute | solution.py:22
  96.1 1.4 collective-permute-start.19
  99.0 1.4 collective-permute-start.21
  100.4 6.1 %convolution_convert_fusion.2 = bf16[3584,1024]{1,0:T(8,128)(2,1)} fusion(bf16[384,3584]{1,0:T(8,128)(2,1)S(1)} %copy-done.2, bf16[384,1024]{1,0:T(8,128)(2,1)S(1)} %get-tuple-element.171), kind=kOutput, calls=%fused_computation.2 | convolution fusion | flops 2822242304 | bytes 10878976 | tf_op jit(solution)/shard_map/dot_general | solution.py:30
  107.5 3.9 %collective-permute-done.19 = bf16[48,1920]{1,0:T(8,128)(2,1)S(1)} collective-permute-done((bf16[48,1920]{1,0:T(8,128)(2,1)S(1)}, bf16[48,1920]{1,0:T(8,128)(2,1)S(1)}, u32[]{:S(2)}, u32[]{:S(2)}) %collective-permute-start.19) | collective-permute-done | bytes 184352 | tf_op jit(solution)/shard_map/ppermute | solution.py:22
  112.4 6.1 %fusion.4 = bf16[1,3584,1024]{2,1,0:T(8,128)(2,1)} fusion(bf16[384,3584]{1,0:T(8,128)(2,1)S(1)} %copy-done.2, bf16[384,1024]{1,0:T(8,128)(2,1)S(1)} %multiply_convert_fusion), kind=kOutput, calls=%fused_computation.7 | convolution fusion | flops 2822242304 | bytes 10878976 | tf_op jit(solution)/shard_map/dot_general | solution.py:30
  118.5 6.2 %fusion.5 = bf16[1,1024,3584]{2,1,0:T(8,128)(2,1)} fusion(bf16[384,1024]{1,0:T(8,128)(2,1)S(1)} %get-tuple-element.194, bf16[384,2688]{1,0:T(8,128)(2,1)S(1)} %constant_dynamic-update-slice_fusion.1, bf16[384,896]{1,0:T(8,128)(2,1)S(1)} %slice.258), kind=kOutput, calls=%fused_computation.8 | convolution fusion | flops 2827747328 | bytes 10878976 | tf_op jit(solution)/shard_map/dot_general | solution.py:30
  124.7 18.1 %collective-permute-done.23 = bf16[128,1920]{1,0:T(8,128)(2,1)S(1)} collective-permute-done((bf16[128,1920]{1,0:T(8,128)(2,1)S(1)}, bf16[128,1920]{1,0:T(8,128)(2,1)S(1)}, u32[]{:S(2)}, u32[]{:S(2)}) %collective-permute-start.23) | collective-permute-done | bytes 491552 | tf_op jit(solution)/shard_map/ppermute | solution.py:22
  (147 shorter events, 24.8 us)
Async XLA Ops:
  0.6 9.7 %copy-start.4 = (s32[1,128,2]{1,2,0:T(2,128)S(1)}, s32[1,128,2]{1,2,0:T(2,128)}, u32[]{:S(2)}) copy-start(s32[1,128,2]{1,2,0:T(2,128)} %param.9) | copy-start | bytes 3076
  0.6 9.7 %copy-start.5 = (f32[1,128,2]{1,2,0:T(2,128)S(1)}, f32[1,128,2]{1,2,0:T(2,128)}, u32[]{:S(2)}) copy-start(f32[1,128,2]{1,2,0:T(2,128)} %param.10) | copy-start | bytes 3076
  0.7 17.8 %copy-start = (bf16[1,384,3584]{2,1,0:T(8,128)(2,1)S(1)}, bf16[1,384,3584]{2,1,0:T(8,128)(2,1)}, u32[]{:S(2)}) copy-start(bf16[1,384,3584]{2,1,0:T(8,128)(2,1)} %param.14) | copy-start | bytes 8257540
  1.8 10.0 %collective-permute-start = (bf16[128,896]{1,0:T(8,128)(2,1)S(1)}, bf16[128,896]{1,0:T(8,128)(2,1)}, u32[]{:S(2)}, u32[]{:S(2)}) collective-permute-start(bf16[128,896]{1,0:T(8,128)(2,1)S(1)} %slice_bitcast_fusion.2), channel_id=1, source_target_pairs={{0,24},{8,0},{16,8},{24,16},{1,25},{9,1},{17,9},{25,17},{2,26},{10... | collective-permute-start | bytes 688136 | tf_op jit(solution)/shard_map/ppermute | solution.py:18
  7.7 19.7 %collective-permute-start.2 = (bf16[128,2688]{1,0:T(8,128)(2,1)}, bf16[128,2688]{1,0:T(8,128)(2,1)}, u32[]{:S(2)}, u32[]{:S(2)}) collective-permute-start(bf16[128,2688]{1,0:T(8,128)(2,1)} %slice_bitcast_fusion.1), channel_id=1, source_target_pairs={{0,24},{8,0},{16,8},{24,16},{1,25},{9,1},{17,9},{25,17},{2,26},{10... | collective-permute-start | bytes 2064392 | tf_op jit(solution)/shard_map/ppermute | solution.py:18
  13.2 9.3 %collective-permute-start.4 = (f32[2,8,128]{2,1,0:T(8,128)S(1)}, f32[2,8,128]{2,1,0:T(8,128)S(1)}, u32[]{:S(2)}, u32[]{:S(2)}) collective-permute-start(f32[2,8,128]{2,1,0:T(8,128)S(1)} %pad_maximum_fusion.10), channel_id=1, source_target_pairs={{0,4},{1,5},{2,6},{3,7},{4,0},{5,1},{6,2},{7,3},{8,12},{9,13},{10,... | collective-permute-start | bytes 24584 | tf_op jit(solution)/shard_map/ppermute | solution.py:22
  15.8 11.5 %collective-permute-start.1 = (bf16[128,896]{1,0:T(8,128)(2,1)}, bf16[128,896]{1,0:T(8,128)(2,1)}, u32[]{:S(2)}, u32[]{:S(2)}) collective-permute-start(bf16[128,896]{1,0:T(8,128)(2,1)} %collective-permute-done), channel_id=1, source_target_pairs={{0,4},{1,5},{2,6},{3,7},{4,0},{5,1},{6,2},{7,3},{8,12},{9,13},{10,... | collective-permute-start | bytes 688136 | tf_op jit(solution)/shard_map/ppermute | solution.py:22
  16.8 8.1 %collective-permute-start.3 = (bf16[96,1024]{1,0:T(8,128)(2,1)}, bf16[96,1024]{1,0:T(8,128)(2,1)}, u32[]{:S(2)}, u32[]{:S(2)}) collective-permute-start(bf16[96,1024]{1,0:T(8,128)(2,1)} %slice.195), channel_id=1, source_target_pairs={{0,2},{1,3},{2,0},{3,1},{4,6},{5,7},{6,4},{7,5},{8,10},{9,11},{10,... | collective-permute-start | bytes 589832 | tf_op jit(solution)/shard_map/ppermute | solution.py:22
  27.4 35.9 %collective-permute-start.5 = (bf16[128,2688]{1,0:T(8,128)(2,1)}, bf16[128,2688]{1,0:T(8,128)(2,1)S(1)}, u32[]{:S(2)}, u32[]{:S(2)}) collective-permute-start(bf16[128,2688]{1,0:T(8,128)(2,1)} %collective-permute-done.2), channel_id=1, source_target_pairs={{0,4},{1,5},{2,6},{3,7},{4,0},{5,1},{6,2},{7,3},{8,12},{9,13},{10,... | collective-permute-start | bytes 2064392 | tf_op jit(solution)/shard_map/ppermute | solution.py:22
  29.5 5.2 %copy-start.2 = (bf16[384,3584]{1,0:T(8,128)(2,1)S(1)}, bf16[384,3584]{1,0:T(8,128)(2,1)}, u32[]{:S(2)}) copy-start(bf16[384,3584]{1,0:T(8,128)(2,1)} %copy-done.1) | copy-start | bytes 8257540
  29.5 19.1 %collective-permute-start.6 = (bf16[96,1024]{1,0:T(8,128)(2,1)S(1)}, bf16[96,1024]{1,0:T(8,128)(2,1)S(1)}, u32[]{:S(2)}, u32[]{:S(2)}) collective-permute-start(bf16[96,1024]{1,0:T(8,128)(2,1)S(1)} %slice.198), channel_id=1, source_target_pairs={{0,2},{1,3},{2,0},{3,1},{4,6},{5,7},{6,4},{7,5},{8,10},{9,11},{10,... | collective-permute-start | bytes 589832 | tf_op jit(solution)/shard_map/ppermute | solution.py:22
  34.3 9.0 %collective-permute-start.8 = (bf16[96,1024]{1,0:T(8,128)(2,1)S(1)}, bf16[96,1024]{1,0:T(8,128)(2,1)S(1)}, u32[]{:S(2)}, u32[]{:S(2)}) collective-permute-start(bf16[96,1024]{1,0:T(8,128)(2,1)S(1)} %pad_maximum_fusion.8), channel_id=1, source_target_pairs={{0,1},{1,0},{2,3},{3,2},{4,5},{5,4},{6,7},{7,6},{8,9},{9,8},{10,11... | collective-permute-start | bytes 589832 | tf_op jit(solution)/shard_map/ppermute | solution.py:22
  34.4 5.9 %slice-start.6 = ((s8[7340032]{0:T(1024)(128)(4,1)}), s8[4194304]{0:T(1024)(128)(4,1)S(1)}, s32[]{:S(2)}) async-start(s8[7340032]{0:T(1024)(128)(4,1)} %bitcast.131), calls=%async_computation.6 | async-start | bytes 8388608
  34.4 5.9 %slice-start.7 = ((s8[7340032]{0:T(1024)(128)(4,1)}), s8[3145728]{0:T(1024)(128)(4,1)S(1)}, s32[]{:S(2)}) async-start(s8[7340032]{0:T(1024)(128)(4,1)} %bitcast.131), calls=%async_computation.7 | async-start | bytes 6291456
  34.5 28.8 %collective-permute-start.7 = (bf16[96,2688]{1,0:T(8,128)(2,1)S(1)}, bf16[96,2688]{1,0:T(8,128)(2,1)S(1)}, u32[]{:S(2)}, u32[]{:S(2)}) collective-permute-start(bf16[96,2688]{1,0:T(8,128)(2,1)S(1)} %slice.199), channel_id=1, source_target_pairs={{0,2},{1,3},{2,0},{3,1},{4,6},{5,7},{6,4},{7,5},{8,10},{9,11},{10,... | collective-permute-start | bytes 1548296 | tf_op jit(solution)/shard_map/ppermute | solution.py:22
  63.8 8.6 %collective-permute-start.11 = (bf16[48,2688]{1,0:T(8,128)(2,1)S(1)}, bf16[48,2688]{1,0:T(8,128)(2,1)S(1)}, u32[]{:S(2)}, u32[]{:S(2)}) collective-permute-start(bf16[48,2688]{1,0:T(8,128)(2,1)S(1)} %get-tuple-element.215), channel_id=1, source_target_pairs={{0,3},{1,2},{2,1},{3,0},{4,7},{5,6},{6,5},{7,4},{8,11},{9,10},{10,... | collective-permute-start | bytes 774152 | tf_op jit(solution)/shard_map/ppermute | solution.py:22
  63.9 13.8 %collective-permute-start.10 = (bf16[48,2688]{1,0:T(8,128)(2,1)S(1)}, bf16[48,2688]{1,0:T(8,128)(2,1)S(1)}, u32[]{:S(2)}, u32[]{:S(2)}) collective-permute-start(bf16[48,2688]{1,0:T(8,128)(2,1)S(1)} %get-tuple-element.216), channel_id=1, source_target_pairs={{0,2},{1,3},{2,0},{3,1},{4,6},{5,7},{6,4},{7,5},{8,10},{9,11},{10,... | collective-permute-start | bytes 774152 | tf_op jit(solution)/shard_map/ppermute | solution.py:22
  65.2 12.5 %collective-permute-start.9 = (bf16[48,2688]{1,0:T(8,128)(2,1)S(1)}, bf16[48,2688]{1,0:T(8,128)(2,1)S(1)}, u32[]{:S(2)}, u32[]{:S(2)}) collective-permute-start(bf16[48,2688]{1,0:T(8,128)(2,1)S(1)} %get-tuple-element.217), channel_id=1, source_target_pairs={{0,1},{1,0},{2,3},{3,2},{4,5},{5,4},{6,7},{7,6},{8,9},{9,8},{10,11... | collective-permute-start | bytes 774152 | tf_op jit(solution)/shard_map/ppermute | solution.py:22
  65.8 1.5 %collective-permute-start.13 = (bf16[96,1024]{1,0:T(8,128)(2,1)S(1)}, bf16[96,1024]{1,0:T(8,128)(2,1)S(1)}, u32[]{:S(2)}, u32[]{:S(2)}) collective-permute-start(bf16[96,1024]{1,0:T(8,128)(2,1)S(1)} %pad_maximum_fusion.9), channel_id=1, source_target_pairs={{0,1},{1,0},{2,3},{3,2},{4,5},{5,4},{6,7},{7,6},{8,9},{9,8},{10,11... | collective-permute-start | bytes 589832 | tf_op jit(solution)/shard_map/ppermute | solution.py:22
  66.0 11.7 %collective-permute-start.12 = (bf16[96,2688]{1,0:T(8,128)(2,1)S(1)}, bf16[96,2688]{1,0:T(8,128)(2,1)S(1)}, u32[]{:S(2)}, u32[]{:S(2)}) collective-permute-start(bf16[96,2688]{1,0:T(8,128)(2,1)S(1)} %pad_maximum_fusion.4), channel_id=1, source_target_pairs={{0,1},{1,0},{2,3},{3,2},{4,5},{5,4},{6,7},{7,6},{8,9},{9,8},{10,11... | collective-permute-start | bytes 1548296 | tf_op jit(solution)/shard_map/ppermute | solution.py:22
  85.6 6.5 %collective-permute-start.16 = (bf16[48,1792]{1,0:T(8,128)(2,1)S(1)}, bf16[48,1792]{1,0:T(8,128)(2,1)S(1)}, u32[]{:S(2)}, u32[]{:S(2)}) collective-permute-start(bf16[48,1792]{1,0:T(8,128)(2,1)S(1)} %get-tuple-element.209), channel_id=1, source_target_pairs={{0,3},{1,2},{2,1},{3,0},{4,7},{5,6},{6,5},{7,4},{8,11},{9,10},{10,... | collective-permute-start | bytes 516104 | tf_op jit(solution)/shard_map/ppermute | solution.py:22
  85.7 10.3 %collective-permute-start.15 = (bf16[48,1792]{1,0:T(8,128)(2,1)S(1)}, bf16[48,1792]{1,0:T(8,128)(2,1)S(1)}, u32[]{:S(2)}, u32[]{:S(2)}) collective-permute-start(bf16[48,1792]{1,0:T(8,128)(2,1)S(1)} %get-tuple-element.210), channel_id=1, source_target_pairs={{0,2},{1,3},{2,0},{3,1},{4,6},{5,7},{6,4},{7,5},{8,10},{9,11},{10,... | collective-permute-start | bytes 516104 | tf_op jit(solution)/shard_map/ppermute | solution.py:22
  87.4 8.6 %collective-permute-start.14 = (bf16[48,1792]{1,0:T(8,128)(2,1)S(1)}, bf16[48,1792]{1,0:T(8,128)(2,1)S(1)}, u32[]{:S(2)}, u32[]{:S(2)}) collective-permute-start(bf16[48,1792]{1,0:T(8,128)(2,1)S(1)} %get-tuple-element.211), channel_id=1, source_target_pairs={{0,1},{1,0},{2,3},{3,2},{4,5},{5,4},{6,7},{7,6},{8,9},{9,8},{10,11... | collective-permute-start | bytes 516104 | tf_op jit(solution)/shard_map/ppermute | solution.py:22
  91.5 4.5 %collective-permute-start.17 = (bf16[96,3712]{1,0:T(8,128)(2,1)S(1)}, bf16[96,3712]{1,0:T(8,128)(2,1)S(1)}, u32[]{:S(2)}, u32[]{:S(2)}) collective-permute-start(bf16[96,3712]{1,0:T(8,128)(2,1)S(1)} %pad_maximum_fusion.2), channel_id=1, source_target_pairs={{0,1},{1,0},{2,3},{3,2},{4,5},{5,4},{6,7},{7,6},{8,9},{9,8},{10,11... | collective-permute-start | bytes 2138120 | tf_op jit(solution)/shard_map/ppermute | solution.py:22
  92.0 6.0 %copy-start.3 = (bf16[192,3712]{1,0:T(8,128)(2,1)}, bf16[192,3712]{1,0:T(8,128)(2,1)S(1)}, u32[]{:S(2)}) copy-start(bf16[192,3712]{1,0:T(8,128)(2,1)S(1)} %pad_maximum_fusion.1) | copy-start | bytes 4276228
  96.1 11.4 %collective-permute-start.20 = (bf16[48,1920]{1,0:T(8,128)(2,1)S(1)}, bf16[48,1920]{1,0:T(8,128)(2,1)S(1)}, u32[]{:S(2)}, u32[]{:S(2)}) collective-permute-start(bf16[48,1920]{1,0:T(8,128)(2,1)S(1)} %get-tuple-element.203), channel_id=1, source_target_pairs={{0,3},{1,2},{2,1},{3,0},{4,7},{5,6},{6,5},{7,4},{8,11},{9,10},{10,... | collective-permute-start | bytes 552968 | tf_op jit(solution)/shard_map/ppermute | solution.py:22
  96.1 15.3 %collective-permute-start.19 = (bf16[48,1920]{1,0:T(8,128)(2,1)S(1)}, bf16[48,1920]{1,0:T(8,128)(2,1)S(1)}, u32[]{:S(2)}, u32[]{:S(2)}) collective-permute-start(bf16[48,1920]{1,0:T(8,128)(2,1)S(1)} %get-tuple-element.204), channel_id=1, source_target_pairs={{0,2},{1,3},{2,0},{3,1},{4,6},{5,7},{6,4},{7,5},{8,10},{9,11},{10,... | collective-permute-start | bytes 552968 | tf_op jit(solution)/shard_map/ppermute | solution.py:22
  97.6 13.8 %collective-permute-start.18 = (bf16[48,1920]{1,0:T(8,128)(2,1)S(1)}, bf16[48,1920]{1,0:T(8,128)(2,1)S(1)}, u32[]{:S(2)}, u32[]{:S(2)}) collective-permute-start(bf16[48,1920]{1,0:T(8,128)(2,1)S(1)} %get-tuple-element.205), channel_id=1, source_target_pairs={{0,1},{1,0},{2,3},{3,2},{4,5},{5,4},{6,7},{7,6},{8,9},{9,8},{10,11... | collective-permute-start | bytes 552968 | tf_op jit(solution)/shard_map/ppermute | solution.py:22
  98.3 26.4 %collective-permute-start.22 = (bf16[128,1792]{1,0:T(8,128)(2,1)S(1)}, bf16[128,1792]{1,0:T(8,128)(2,1)S(1)}, u32[]{:S(2)}, u32[]{:S(2)}) collective-permute-start(bf16[128,1792]{1,0:T(8,128)(2,1)S(1)} %convolution_convert_fusion.6), channel_id=1, source_target_pairs={{0,4},{1,5},{2,6},{3,7},{4,0},{5,1},{6,2},{7,3},{8,12},{9,13},{10,... | collective-permute-start | bytes 1376264 | tf_op jit(solution)/shard_map/ppermute | solution.py:22
  99.0 43.8 %collective-permute-start.21 = (bf16[96,3712]{1,0:T(8,128)(2,1)S(1)}, bf16[96,3712]{1,0:T(8,128)(2,1)S(1)}, u32[]{:S(2)}, u32[]{:S(2)}) collective-permute-start(bf16[96,3712]{1,0:T(8,128)(2,1)S(1)} %pad_maximum_fusion.3), channel_id=1, source_target_pairs={{0,2},{1,3},{2,0},{3,1},{4,6},{5,7},{6,4},{7,5},{8,10},{9,11},{10,... | collective-permute-start | bytes 2138120 | tf_op jit(solution)/shard_map/ppermute | solution.py:22
  111.7 31.0 %collective-permute-start.23 = (bf16[128,1920]{1,0:T(8,128)(2,1)S(1)}, bf16[128,1920]{1,0:T(8,128)(2,1)S(1)}, u32[]{:S(2)}, u32[]{:S(2)}) collective-permute-start(bf16[128,1920]{1,0:T(8,128)(2,1)S(1)} %convolution_convert_fusion.5), channel_id=1, source_target_pairs={{0,4},{1,5},{2,6},{3,7},{4,0},{5,1},{6,2},{7,3},{8,12},{9,13},{10,... | collective-permute-start | bytes 1474568 | tf_op jit(solution)/shard_map/ppermute | solution.py:22
  118.5 24.3 %slice-start.1 = ((bf16[192,3712]{1,0:T(8,128)(2,1)}), bf16[48,3712]{1,0:T(8,128)(2,1)S(1)}, s32[]{:S(2)}) async-start(bf16[192,3712]{1,0:T(8,128)(2,1)} %copy-done.3), calls=%async_computation.1 | async-start | bytes 712704 | tf_op jit(solution)/shard_map/slice | solution.py:235
  (8 other events, 19.7 us)

commit v3 on v2

--- a/solution.py
+++ b/solution.py
@@ -213,14 +213,20 @@
     back[1] = jnp.concatenate([back[1], gate_terms(rest[4], rest[3])], axis=1)
     near_back = jnp.concatenate([back[j][:half] for j in range(steps)], axis=1)
     given = swap(stacked(near_back[CAP : 2 * CAP], near_back[3 * CAP :]), 1)
-    hands, back, rest, near_back, given = together(hands, back, rest, near_back, given)
+    far_back = back[1][half:]
+    far_given = swap(stacked(far_back[CAP : 2 * CAP], far_back[3 * CAP :]), 1)
+    hands, back, rest, near_back, given, far_given = together(
+        hands, back, rest, near_back, given, far_given
+    )
+    far_back = back[1][half:]
     near_sent = stacked(near_back[2 * CAP : 3 * CAP], given[CAP:])
 
     def crossing(name, hands):
         far_sum = mm(far_sel, stacked(*hands), ((0,), (0,))).astype(bf16)
         return far_sum
 
-    more = far_hands(1)
+    far_got = swap(stacked(far_back[2 * CAP : 3 * CAP], far_given[CAP:]), 2)
+    more = [far_back[:CAP], far_given[:CAP], far_got[:CAP], far_got[CAP:]]
     far_sum = crossing(0, hands)
     far_sum, rest, near_back = together(far_sum, rest, near_back)
     crossed = [swap(far_sum, 4)]

time: 145 us -> 150 us (1.034)
  waiting for transfers between devices: 60.6 us -> 66.2 us
    ppermute x22 -> x21, waiting for transfers between devices: 59.3 us -> 64.9 us  [swap(): return lax.ppermute(x, EXPERT, [(i, i ^ bit) for i in range(8)])]
    ppermute x22 -> x21, starting transfers between devices: 17.1 us -> 15.9 us  [swap(): return lax.ppermute(x, EXPERT, [(i, i ^ bit) for i in range(8)])]
  transfers between devices with their start and end apart: 24 -> 23, of which waited for: 12 -> 12; matrix products, arithmetic and copies ran while one was open for 31% -> 27% of each run, Pallas kernels for 2% -> 2%
where the time goes in v3:
time: 150 us; the launch traced here: 149 us
  waiting for transfers between devices  66.2 us (44%)
  matrix products  43 us (29%)
  starting transfers between devices  20.3 us (14%)
  local copies, waits for them, and re-layouts  10.5 us (7%)
  other arithmetic  5.22 us (3%)
  Pallas kernels  2.48 us (2%)
    ppermute x21, waiting for transfers between devices, swap(): return lax.ppermute(x, EXPERT, [(i, i ^ bit) for i in range(8)])  64.9 us
    dot_general x21, matrix products, mm(): lax.dot_general(a, b, (dims, ((), ())), preferred_element_type=jnp.float32)  43 us
    ppermute x21, starting transfers between devices, swap(): return lax.ppermute(x, EXPERT, [(i, i ^ bit) for i in range(8)])  15.9 us
    ppermute x2, starting transfers between devices, shifted(): return lax.ppermute(x, axis, [(i, (i + by) % size) for i in range(size)])  4.48 us
    unnamed x39, local copies, waits for them, and re-layouts  4.12 us
    squeeze x2, local copies, waits for them, and re-layouts, relayed(): pieces = [upstream[0, :, lo:hi] for lo, hi in spans]  3.1 us
  transfers between devices with their start and end apart: 23, of which 12 were waited for; matrix products, arithmetic and copies ran while one was open for 27% of the time, Pallas kernels for 2%

profile of v3, /device:TPU:0, one launch (start us, length us, event | category | flops | bytes accessed | tf_op | source)
XLA Modules:
  0.0 149.2 jit_solution(7666749225618994485)
XLA Ops:
  1.8 3.9 %collective-permute-start = (bf16[128,896]{1,0:T(8,128)(2,1)S(1)}, bf16[128,896]{1,0:T(8,128)(2,1)}, u32[]{:S(2)}, u32[]{:S(2)}) collective-permute-start(bf16[128,896]{1,0:T(8,128)(2,1)S(1)} %slice_bitcast_fusion.2), channel_id=1, source_target_pairs={{0,24},{8,0},{16,8},{24,16},{1,25},{9,1},{17,9},{25,17},{2,26},{10... | collective-permute-start | bytes 688136 | tf_op jit(solution)/shard_map/ppermute | solution.py:18
  5.7 2.0 %slice_bitcast_fusion.1 = bf16[128,2688]{1,0:T(8,128)(2,1)} fusion(bf16[1,128,3584]{2,1,0:T(8,128)(2,1)} %param.8), kind=kLoop, calls=%fused_computation.86 | loop fusion | bytes 1376256 | tf_op jit(solution)/shard_map/squeeze | solution.py:87
  10.4 1.3 collective-permute-done
  13.2 2.7 %collective-permute-start.4 = (f32[2,8,128]{2,1,0:T(8,128)S(1)}, f32[2,8,128]{2,1,0:T(8,128)S(1)}, u32[]{:S(2)}, u32[]{:S(2)}) collective-permute-start(f32[2,8,128]{2,1,0:T(8,128)S(1)} %pad_maximum_fusion.12), channel_id=1, source_target_pairs={{0,4},{1,5},{2,6},{3,7},{4,0},{5,1},{6,2},{7,3},{8,12},{9,13},{10,... | collective-permute-start | bytes 24584 | tf_op jit(solution)/shard_map/ppermute | solution.py:22
  16.8 1.6 %collective-permute-start.3 = (bf16[96,1024]{1,0:T(8,128)(2,1)}, bf16[96,1024]{1,0:T(8,128)(2,1)}, u32[]{:S(2)}, u32[]{:S(2)}) collective-permute-start(bf16[96,1024]{1,0:T(8,128)(2,1)} %slice.209), channel_id=1, source_target_pairs={{0,2},{1,3},{2,0},{3,1},{4,6},{5,7},{6,4},{7,5},{8,10},{9,11},{10,... | collective-permute-start | bytes 589832 | tf_op jit(solution)/shard_map/ppermute | solution.py:22
  18.4 2.5 %shard_map.119 = bf16[384,3584]{1,0:T(8,128)(2,1)S(1)} custom-call(s32[8]{0:T(128)S(1)} %iota_xor_fusion.order, bf16[384,3584]{1,0:T(8,128)(2,1)S(1)} %bitcast.110, f32[384,28]{1,0:T(8,128)S(1)} %bitcast.114, bf16[384,3584]{1,0:T(8,128)(2,1)S(1)} %bitcast.111, f32[384,28]{1,0:T(8,128)S(1)} %bitcast.115, bf16[384,3584]{1,0:T(8,128)(2,1)S(1)} %bitcast.112, ...), custom_call_target="tpu_custom_call" | custom-call | flops 1 | bytes 1 | tf_op jit(solution)/shard_map/pallas_call | solution.py:57
  20.9 1.5 %copy-done.1 = bf16[384,3584]{1,0:T(8,128)(2,1)} copy-done((bf16[384,3584]{1,0:T(8,128)(2,1)}, bf16[384,3584]{1,0:T(8,128)(2,1)S(1)}, u32[]{:S(2)}) %copy-start.1) | copy-done | bytes 2752536
  22.8 2.2 %collective-permute-done.3 = bf16[96,1024]{1,0:T(8,128)(2,1)} collective-permute-done((bf16[96,1024]{1,0:T(8,128)(2,1)}, bf16[96,1024]{1,0:T(8,128)(2,1)}, u32[]{:S(2)}, u32[]{:S(2)}) %collective-permute-start.3) | collective-permute-done | bytes 196640 | tf_op jit(solution)/shard_map/ppermute | solution.py:22
  25.0 2.4 %collective-permute-done.1 = bf16[128,896]{1,0:T(8,128)(2,1)} collective-permute-done((bf16[128,896]{1,0:T(8,128)(2,1)}, bf16[128,896]{1,0:T(8,128)(2,1)}, u32[]{:S(2)}, u32[]{:S(2)}) %collective-permute-start.1) | collective-permute-done | bytes 229408 | tf_op jit(solution)/shard_map/ppermute | solution.py:22
  29.5 2.3 %collective-permute-start.6 = (bf16[96,1024]{1,0:T(8,128)(2,1)S(1)}, bf16[96,1024]{1,0:T(8,128)(2,1)S(1)}, u32[]{:S(2)}, u32[]{:S(2)}) collective-permute-start(bf16[96,1024]{1,0:T(8,128)(2,1)S(1)} %slice.212), channel_id=1, source_target_pairs={{0,2},{1,3},{2,0},{3,1},{4,6},{5,7},{6,4},{7,5},{8,10},{9,11},{10,... | collective-permute-start | bytes 589832 | tf_op jit(solution)/shard_map/ppermute | solution.py:22
  31.8 1.5 %convolution_convert_fusion.4 = bf16[192,2688]{1,0:T(8,128)(2,1)S(1)} fusion(bf16[192,128]{1,0:T(8,128)(2,1)S(1)} %fusion.64, bf16[128,2688]{1,0:T(8,128)(2,1)} %collective-permute-done.2), kind=kOutput, calls=%fused_computation.14 | convolution fusion | flops 132636672 | bytes 1769472 | tf_op jit(solution)/shard_map/dot_general | solution.py:30
  34.7 5.6 %fusion = f32[384,1024]{1,0:T(8,128)S(1)} fusion(bf16[384,3584]{1,0:T(8,128)(2,1)S(1)} %copy-done.2, bf16[1,3584,1024]{2,1,0:T(8,128)(2,1)} %param.12), kind=kOutput, calls=%fused_computation.3 | convolution fusion | flops 2818572288 | bytes 11665408 | tf_op jit(solution)/shard_map/dot_general | solution.py:30
  40.3 3.0 %fusion.2 = f32[384,1024]{1,0:T(8,128)S(1)} fusion(bf16[384,3584]{1,0:T(8,128)(2,1)S(1)} %copy-done.2, bf16[1,3584,1024]{2,1,0:T(8,128)(2,1)S(1)} %bitcast.132), kind=kOutput, calls=%fused_computation.5 | convolution fusion | flops 2818572288 | bytes 11665408 | tf_op jit(solution)/shard_map/dot_general | solution.py:30
  43.4 5.1 %collective-permute-done.6 = bf16[96,1024]{1,0:T(8,128)(2,1)S(1)} collective-permute-done((bf16[96,1024]{1,0:T(8,128)(2,1)S(1)}, bf16[96,1024]{1,0:T(8,128)(2,1)S(1)}, u32[]{:S(2)}, u32[]{:S(2)}) %collective-permute-start.6) | collective-permute-done | bytes 196640 | tf_op jit(solution)/shard_map/ppermute | solution.py:22
  48.5 14.8 %collective-permute-done.7 = bf16[96,2688]{1,0:T(8,128)(2,1)S(1)} collective-permute-done((bf16[96,2688]{1,0:T(8,128)(2,1)S(1)}, bf16[96,2688]{1,0:T(8,128)(2,1)S(1)}, u32[]{:S(2)}, u32[]{:S(2)}) %collective-permute-start.7) | collective-permute-done | bytes 516128 | tf_op jit(solution)/shard_map/ppermute | solution.py:22
  63.9 1.3 collective-permute-start.10
  70.6 1.8 %collective-permute-done.11 = bf16[48,2688]{1,0:T(8,128)(2,1)S(1)} collective-permute-done((bf16[48,2688]{1,0:T(8,128)(2,1)S(1)}, bf16[48,2688]{1,0:T(8,128)(2,1)S(1)}, u32[]{:S(2)}, u32[]{:S(2)}) %collective-permute-start.11) | collective-permute-done | bytes 258080 | tf_op jit(solution)/shard_map/ppermute | solution.py:22
  72.4 5.3 %collective-permute-done.10 = bf16[48,2688]{1,0:T(8,128)(2,1)S(1)} collective-permute-done((bf16[48,2688]{1,0:T(8,128)(2,1)S(1)}, bf16[48,2688]{1,0:T(8,128)(2,1)S(1)}, u32[]{:S(2)}, u32[]{:S(2)}) %collective-permute-start.10) | collective-permute-done | bytes 258080 | tf_op jit(solution)/shard_map/ppermute | solution.py:22
  77.9 2.4 %fusion.6 = f32[384,1024]{1,0:T(8,128)S(1)} fusion(bf16[384,2688]{1,0:T(8,128)(2,1)S(1)} %constant_dynamic-update-slice_fusion.1, bf16[1024,3584]{1,0:T(8,128)(2,1)S(1)} %bitcast.128), kind=kOutput, calls=%fused_computation.9 | convolution fusion | flops 2113929216 | bytes 9142272 | tf_op jit(solution)/shard_map/dot_general | solution.py:30
  81.3 1.6 %fusion.13 = f32[384,1792]{1,0:T(8,128)S(1)} fusion(bf16[384,1024]{1,0:T(8,128)(2,1)S(1)} %multiply_convert_fusion, bf16[1,3584,1024]{2,1,0:T(8,128)(2,1)S(1)} %bitcast.130), kind=kOutput, calls=%fused_computation.19 | convolution fusion | flops 1409286144 | bytes 7208960 | tf_op jit(solution)/shard_map/dot_general | solution.py:30
  83.6 1.7 %fusion.30 = bf16[384,1792]{1,0:T(8,128)(2,1)S(1)} fusion(f32[384,1792]{1,0:T(8,128)S(1)} %fusion.13, bf16[384,1024]{1,0:T(8,128)(2,1)S(1)} %get-tuple-element.173, bf16[1,3584,1024]{2,1,0:T(8,128)(2,1)S(1)} %bitcast.134), kind=kOutput, calls=%fused_computation.34 | convolution fusion | flops 1410662400 | bytes 8585216 | tf_op jit(solution)/shard_map/dot_general | solution.py:30
  85.5 1.6 %fusion.9 = f32[384,1792]{1,0:T(8,128)S(1)} fusion(bf16[384,1024]{1,0:T(8,128)(2,1)S(1)} %multiply_convert_fusion, bf16[1,3584,1024]{2,1,0:T(8,128)(2,1)S(1)} %bitcast.130), kind=kOutput, calls=%fused_computation.15 | convolution fusion | flops 1409286144 | bytes 7208960 | tf_op jit(solution)/shard_map/dot_general | solution.py:30
  87.1 1.9 %fusion.27 = bf16[384,1792]{1,0:T(8,128)(2,1)S(1)} fusion(f32[384,1792]{1,0:T(8,128)S(1)} %fusion.9, bf16[384,1024]{1,0:T(8,128)(2,1)S(1)} %get-tuple-element.173, bf16[1,3584,1024]{2,1,0:T(8,128)(2,1)S(1)} %bitcast.134), kind=kOutput, calls=%fused_computation.33 | convolution fusion | flops 1410662400 | bytes 8585216 | tf_op jit(solution)/shard_map/dot_general | solution.py:30
  90.5 1.8 %collective-permute-start.15 = (bf16[48,1792]{1,0:T(8,128)(2,1)S(1)}, bf16[48,1792]{1,0:T(8,128)(2,1)S(1)}, u32[]{:S(2)}, u32[]{:S(2)}) collective-permute-start(bf16[48,1792]{1,0:T(8,128)(2,1)S(1)} %get-tuple-element.212), channel_id=1, source_target_pairs={{0,2},{1,3},{2,0},{3,1},{4,6},{5,7},{6,4},{7,5},{8,10},{9,11},{10,... | collective-permute-start | bytes 516104 | tf_op jit(solution)/shard_map/ppermute | solution.py:22
  92.4 4.4 %collective-permute-done.16 = bf16[48,1792]{1,0:T(8,128)(2,1)S(1)} collective-permute-done((bf16[48,1792]{1,0:T(8,128)(2,1)S(1)}, bf16[48,1792]{1,0:T(8,128)(2,1)S(1)}, u32[]{:S(2)}, u32[]{:S(2)}) %collective-permute-start.16) | collective-permute-done | bytes 172064 | tf_op jit(solution)/shard_map/ppermute | solution.py:22
  96.8 4.0 %collective-permute-done.15 = bf16[48,1792]{1,0:T(8,128)(2,1)S(1)} collective-permute-done((bf16[48,1792]{1,0:T(8,128)(2,1)S(1)}, bf16[48,1792]{1,0:T(8,128)(2,1)S(1)}, u32[]{:S(2)}, u32[]{:S(2)}) %collective-permute-start.15) | collective-permute-done | bytes 172064 | tf_op jit(solution)/shard_map/ppermute | solution.py:22
  101.4 1.9 %collective-permute-start.21 = (bf16[128,1792]{1,0:T(8,128)(2,1)S(1)}, bf16[128,1792]{1,0:T(8,128)(2,1)S(1)}, u32[]{:S(2)}, u32[]{:S(2)}) collective-permute-start(bf16[128,1792]{1,0:T(8,128)(2,1)S(1)} %convolution_convert_fusion.6), channel_id=1, source_target_pairs={{0,4},{1,5},{2,6},{3,7},{4,0},{5,1},{6,2},{7,3},{8,12},{9,13},{10,... | collective-permute-start | bytes 1376264 | tf_op jit(solution)/shard_map/ppermute | solution.py:22
  103.6 6.1 %convolution_convert_fusion.2 = bf16[3584,1024]{1,0:T(8,128)(2,1)} fusion(bf16[384,3584]{1,0:T(8,128)(2,1)S(1)} %copy-done.2, bf16[384,1024]{1,0:T(8,128)(2,1)S(1)} %get-tuple-element.173), kind=kOutput, calls=%fused_computation.2 | convolution fusion | flops 2822242304 | bytes 10878976 | tf_op jit(solution)/shard_map/dot_general | solution.py:30
  109.7 9.0 %collective-permute-done.19 = bf16[96,1920]{1,0:T(8,128)(2,1)S(1)} collective-permute-done((bf16[96,1920]{1,0:T(8,128)(2,1)S(1)}, bf16[96,1920]{1,0:T(8,128)(2,1)S(1)}, u32[]{:S(2)}, u32[]{:S(2)}) %collective-permute-start.19) | collective-permute-done | bytes 368672 | tf_op jit(solution)/shard_map/ppermute | solution.py:22
  119.6 6.1 %fusion.4 = bf16[1,3584,1024]{2,1,0:T(8,128)(2,1)} fusion(bf16[384,3584]{1,0:T(8,128)(2,1)S(1)} %copy-done.2, bf16[384,1024]{1,0:T(8,128)(2,1)S(1)} %multiply_convert_fusion), kind=kOutput, calls=%fused_computation.7 | convolution fusion | flops 2822242304 | bytes 10878976 | tf_op jit(solution)/shard_map/dot_general | solution.py:30
  125.7 6.2 %fusion.5 = bf16[1,1024,3584]{2,1,0:T(8,128)(2,1)} fusion(bf16[384,1024]{1,0:T(8,128)(2,1)S(1)} %get-tuple-element.196, bf16[384,2688]{1,0:T(8,128)(2,1)S(1)} %constant_dynamic-update-slice_fusion.1, bf16[384,896]{1,0:T(8,128)(2,1)S(1)} %slice.276), kind=kOutput, calls=%fused_computation.8 | convolution fusion | flops 2827747328 | bytes 10878976 | tf_op jit(solution)/shard_map/dot_general | solution.py:30
  131.9 15.1 %collective-permute-done.20 = bf16[96,3712]{1,0:T(8,128)(2,1)S(1)} collective-permute-done((bf16[96,3712]{1,0:T(8,128)(2,1)S(1)}, bf16[96,3712]{1,0:T(8,128)(2,1)S(1)}, u32[]{:S(2)}, u32[]{:S(2)}) %collective-permute-start.20) | collective-permute-done | bytes 712736 | tf_op jit(solution)/shard_map/ppermute | solution.py:22
  (150 shorter events, 23.2 us)
Async XLA Ops:
  0.6 9.7 %copy-start.4 = (s32[1,128,2]{1,2,0:T(2,128)S(1)}, s32[1,128,2]{1,2,0:T(2,128)}, u32[]{:S(2)}) copy-start(s32[1,128,2]{1,2,0:T(2,128)} %param.9) | copy-start | bytes 3076
  0.6 9.7 %copy-start.5 = (f32[1,128,2]{1,2,0:T(2,128)S(1)}, f32[1,128,2]{1,2,0:T(2,128)}, u32[]{:S(2)}) copy-start(f32[1,128,2]{1,2,0:T(2,128)} %param.10) | copy-start | bytes 3076
  0.7 17.8 %copy-start = (bf16[1,384,3584]{2,1,0:T(8,128)(2,1)S(1)}, bf16[1,384,3584]{2,1,0:T(8,128)(2,1)}, u32[]{:S(2)}) copy-start(bf16[1,384,3584]{2,1,0:T(8,128)(2,1)} %param.14) | copy-start | bytes 8257540
  1.8 10.0 %collective-permute-start = (bf16[128,896]{1,0:T(8,128)(2,1)S(1)}, bf16[128,896]{1,0:T(8,128)(2,1)}, u32[]{:S(2)}, u32[]{:S(2)}) collective-permute-start(bf16[128,896]{1,0:T(8,128)(2,1)S(1)} %slice_bitcast_fusion.2), channel_id=1, source_target_pairs={{0,24},{8,0},{16,8},{24,16},{1,25},{9,1},{17,9},{25,17},{2,26},{10... | collective-permute-start | bytes 688136 | tf_op jit(solution)/shard_map/ppermute | solution.py:18
  7.7 19.7 %collective-permute-start.2 = (bf16[128,2688]{1,0:T(8,128)(2,1)}, bf16[128,2688]{1,0:T(8,128)(2,1)}, u32[]{:S(2)}, u32[]{:S(2)}) collective-permute-start(bf16[128,2688]{1,0:T(8,128)(2,1)} %slice_bitcast_fusion.1), channel_id=1, source_target_pairs={{0,24},{8,0},{16,8},{24,16},{1,25},{9,1},{17,9},{25,17},{2,26},{10... | collective-permute-start | bytes 2064392 | tf_op jit(solution)/shard_map/ppermute | solution.py:18
  13.2 9.3 %collective-permute-start.4 = (f32[2,8,128]{2,1,0:T(8,128)S(1)}, f32[2,8,128]{2,1,0:T(8,128)S(1)}, u32[]{:S(2)}, u32[]{:S(2)}) collective-permute-start(f32[2,8,128]{2,1,0:T(8,128)S(1)} %pad_maximum_fusion.12), channel_id=1, source_target_pairs={{0,4},{1,5},{2,6},{3,7},{4,0},{5,1},{6,2},{7,3},{8,12},{9,13},{10,... | collective-permute-start | bytes 24584 | tf_op jit(solution)/shard_map/ppermute | solution.py:22
  15.8 11.5 %collective-permute-start.1 = (bf16[128,896]{1,0:T(8,128)(2,1)}, bf16[128,896]{1,0:T(8,128)(2,1)}, u32[]{:S(2)}, u32[]{:S(2)}) collective-permute-start(bf16[128,896]{1,0:T(8,128)(2,1)} %collective-permute-done), channel_id=1, source_target_pairs={{0,4},{1,5},{2,6},{3,7},{4,0},{5,1},{6,2},{7,3},{8,12},{9,13},{10,... | collective-permute-start | bytes 688136 | tf_op jit(solution)/shard_map/ppermute | solution.py:22
  16.8 8.1 %collective-permute-start.3 = (bf16[96,1024]{1,0:T(8,128)(2,1)}, bf16[96,1024]{1,0:T(8,128)(2,1)}, u32[]{:S(2)}, u32[]{:S(2)}) collective-permute-start(bf16[96,1024]{1,0:T(8,128)(2,1)} %slice.209), channel_id=1, source_target_pairs={{0,2},{1,3},{2,0},{3,1},{4,6},{5,7},{6,4},{7,5},{8,10},{9,11},{10,... | collective-permute-start | bytes 589832 | tf_op jit(solution)/shard_map/ppermute | solution.py:22
  27.4 35.9 %collective-permute-start.5 = (bf16[128,2688]{1,0:T(8,128)(2,1)}, bf16[128,2688]{1,0:T(8,128)(2,1)S(1)}, u32[]{:S(2)}, u32[]{:S(2)}) collective-permute-start(bf16[128,2688]{1,0:T(8,128)(2,1)} %collective-permute-done.2), channel_id=1, source_target_pairs={{0,4},{1,5},{2,6},{3,7},{4,0},{5,1},{6,2},{7,3},{8,12},{9,13},{10,... | collective-permute-start | bytes 2064392 | tf_op jit(solution)/shard_map/ppermute | solution.py:22
  29.5 5.2 %copy-start.2 = (bf16[384,3584]{1,0:T(8,128)(2,1)S(1)}, bf16[384,3584]{1,0:T(8,128)(2,1)}, u32[]{:S(2)}) copy-start(bf16[384,3584]{1,0:T(8,128)(2,1)} %copy-done.1) | copy-start | bytes 8257540
  29.5 19.1 %collective-permute-start.6 = (bf16[96,1024]{1,0:T(8,128)(2,1)S(1)}, bf16[96,1024]{1,0:T(8,128)(2,1)S(1)}, u32[]{:S(2)}, u32[]{:S(2)}) collective-permute-start(bf16[96,1024]{1,0:T(8,128)(2,1)S(1)} %slice.212), channel_id=1, source_target_pairs={{0,2},{1,3},{2,0},{3,1},{4,6},{5,7},{6,4},{7,5},{8,10},{9,11},{10,... | collective-permute-start | bytes 589832 | tf_op jit(solution)/shard_map/ppermute | solution.py:22
  34.3 9.0 %collective-permute-start.8 = (bf16[96,1024]{1,0:T(8,128)(2,1)S(1)}, bf16[96,1024]{1,0:T(8,128)(2,1)S(1)}, u32[]{:S(2)}, u32[]{:S(2)}) collective-permute-start(bf16[96,1024]{1,0:T(8,128)(2,1)S(1)} %pad_maximum_fusion.10), channel_id=1, source_target_pairs={{0,1},{1,0},{2,3},{3,2},{4,5},{5,4},{6,7},{7,6},{8,9},{9,8},{10,11... | collective-permute-start | bytes 589832 | tf_op jit(solution)/shard_map/ppermute | solution.py:22
  34.4 5.9 %slice-start.6 = ((s8[7340032]{0:T(1024)(128)(4,1)}), s8[4194304]{0:T(1024)(128)(4,1)S(1)}, s32[]{:S(2)}) async-start(s8[7340032]{0:T(1024)(128)(4,1)} %bitcast.131), calls=%async_computation.6 | async-start | bytes 8388608
  34.4 5.9 %slice-start.7 = ((s8[7340032]{0:T(1024)(128)(4,1)}), s8[3145728]{0:T(1024)(128)(4,1)S(1)}, s32[]{:S(2)}) async-start(s8[7340032]{0:T(1024)(128)(4,1)} %bitcast.131), calls=%async_computation.7 | async-start | bytes 6291456
  34.5 28.8 %collective-permute-start.7 = (bf16[96,2688]{1,0:T(8,128)(2,1)S(1)}, bf16[96,2688]{1,0:T(8,128)(2,1)S(1)}, u32[]{:S(2)}, u32[]{:S(2)}) collective-permute-start(bf16[96,2688]{1,0:T(8,128)(2,1)S(1)} %slice.213), channel_id=1, source_target_pairs={{0,2},{1,3},{2,0},{3,1},{4,6},{5,7},{6,4},{7,5},{8,10},{9,11},{10,... | collective-permute-start | bytes 1548296 | tf_op jit(solution)/shard_map/ppermute | solution.py:22
  63.8 8.6 %collective-permute-start.11 = (bf16[48,2688]{1,0:T(8,128)(2,1)S(1)}, bf16[48,2688]{1,0:T(8,128)(2,1)S(1)}, u32[]{:S(2)}, u32[]{:S(2)}) collective-permute-start(bf16[48,2688]{1,0:T(8,128)(2,1)S(1)} %get-tuple-element.217), channel_id=1, source_target_pairs={{0,3},{1,2},{2,1},{3,0},{4,7},{5,6},{6,5},{7,4},{8,11},{9,10},{10,... | collective-permute-start | bytes 774152 | tf_op jit(solution)/shard_map/ppermute | solution.py:22
  63.9 13.8 %collective-permute-start.10 = (bf16[48,2688]{1,0:T(8,128)(2,1)S(1)}, bf16[48,2688]{1,0:T(8,128)(2,1)S(1)}, u32[]{:S(2)}, u32[]{:S(2)}) collective-permute-start(bf16[48,2688]{1,0:T(8,128)(2,1)S(1)} %get-tuple-element.218), channel_id=1, source_target_pairs={{0,2},{1,3},{2,0},{3,1},{4,6},{5,7},{6,4},{7,5},{8,10},{9,11},{10,... | collective-permute-start | bytes 774152 | tf_op jit(solution)/shard_map/ppermute | solution.py:22
  65.2 12.5 %collective-permute-start.9 = (bf16[48,2688]{1,0:T(8,128)(2,1)S(1)}, bf16[48,2688]{1,0:T(8,128)(2,1)S(1)}, u32[]{:S(2)}, u32[]{:S(2)}) collective-permute-start(bf16[48,2688]{1,0:T(8,128)(2,1)S(1)} %get-tuple-element.219), channel_id=1, source_target_pairs={{0,1},{1,0},{2,3},{3,2},{4,5},{5,4},{6,7},{7,6},{8,9},{9,8},{10,11... | collective-permute-start | bytes 774152 | tf_op jit(solution)/shard_map/ppermute | solution.py:22
  65.8 1.5 %collective-permute-start.13 = (bf16[96,1024]{1,0:T(8,128)(2,1)S(1)}, bf16[96,1024]{1,0:T(8,128)(2,1)S(1)}, u32[]{:S(2)}, u32[]{:S(2)}) collective-permute-start(bf16[96,1024]{1,0:T(8,128)(2,1)S(1)} %pad_maximum_fusion.11), channel_id=1, source_target_pairs={{0,1},{1,0},{2,3},{3,2},{4,5},{5,4},{6,7},{7,6},{8,9},{9,8},{10,11... | collective-permute-start | bytes 589832 | tf_op jit(solution)/shard_map/ppermute | solution.py:22
  66.0 11.7 %collective-permute-start.12 = (bf16[96,2688]{1,0:T(8,128)(2,1)S(1)}, bf16[96,2688]{1,0:T(8,128)(2,1)S(1)}, u32[]{:S(2)}, u32[]{:S(2)}) collective-permute-start(bf16[96,2688]{1,0:T(8,128)(2,1)S(1)} %pad_maximum_fusion.4), channel_id=1, source_target_pairs={{0,1},{1,0},{2,3},{3,2},{4,5},{5,4},{6,7},{7,6},{8,9},{9,8},{10,11... | collective-permute-start | bytes 1548296 | tf_op jit(solution)/shard_map/ppermute | solution.py:22
  77.8 3.5 %slice-start.4 = ((s8[7340032]{0:T(1024)(128)(4,1)}), s8[4194304]{0:T(1024)(128)(4,1)S(1)}, s32[]{:S(2)}) async-start(s8[7340032]{0:T(1024)(128)(4,1)} %bitcast.129), calls=%async_computation.4 | async-start | bytes 8388608
  89.6 11.3 %copy-start.3 = (bf16[192,3712]{1,0:T(8,128)(2,1)}, bf16[192,3712]{1,0:T(8,128)(2,1)S(1)}, u32[]{:S(2)}) copy-start(bf16[192,3712]{1,0:T(8,128)(2,1)S(1)} %pad_maximum_fusion.1) | copy-start | bytes 4276228
  89.6 11.2 %collective-permute-start.18 = (bf16[96,1920]{1,0:T(8,128)(2,1)S(1)}, bf16[96,1920]{1,0:T(8,128)(2,1)S(1)}, u32[]{:S(2)}, u32[]{:S(2)}) collective-permute-start(bf16[96,1920]{1,0:T(8,128)(2,1)S(1)} %pad_maximum_fusion.8), channel_id=1, source_target_pairs={{0,1},{1,0},{2,3},{3,2},{4,5},{5,4},{6,7},{7,6},{8,9},{9,8},{10,11... | collective-permute-start | bytes 1105928 | tf_op jit(solution)/shard_map/ppermute | solution.py:22
  89.9 10.9 %collective-permute-start.17 = (bf16[96,3712]{1,0:T(8,128)(2,1)S(1)}, bf16[96,3712]{1,0:T(8,128)(2,1)S(1)}, u32[]{:S(2)}, u32[]{:S(2)}) collective-permute-start(bf16[96,3712]{1,0:T(8,128)(2,1)S(1)} %pad_maximum_fusion.2), channel_id=1, source_target_pairs={{0,1},{1,0},{2,3},{3,2},{4,5},{5,4},{6,7},{7,6},{8,9},{9,8},{10,11... | collective-permute-start | bytes 2138120 | tf_op jit(solution)/shard_map/ppermute | solution.py:22
  90.4 6.4 %collective-permute-start.16 = (bf16[48,1792]{1,0:T(8,128)(2,1)S(1)}, bf16[48,1792]{1,0:T(8,128)(2,1)S(1)}, u32[]{:S(2)}, u32[]{:S(2)}) collective-permute-start(bf16[48,1792]{1,0:T(8,128)(2,1)S(1)} %get-tuple-element.211), channel_id=1, source_target_pairs={{0,3},{1,2},{2,1},{3,0},{4,7},{5,6},{6,5},{7,4},{8,11},{9,10},{10,... | collective-permute-start | bytes 516104 | tf_op jit(solution)/shard_map/ppermute | solution.py:22
  90.5 10.3 %collective-permute-start.15 = (bf16[48,1792]{1,0:T(8,128)(2,1)S(1)}, bf16[48,1792]{1,0:T(8,128)(2,1)S(1)}, u32[]{:S(2)}, u32[]{:S(2)}) collective-permute-start(bf16[48,1792]{1,0:T(8,128)(2,1)S(1)} %get-tuple-element.212), channel_id=1, source_target_pairs={{0,2},{1,3},{2,0},{3,1},{4,6},{5,7},{6,4},{7,5},{8,10},{9,11},{10,... | collective-permute-start | bytes 516104 | tf_op jit(solution)/shard_map/ppermute | solution.py:22
  92.2 8.6 %collective-permute-start.14 = (bf16[48,1792]{1,0:T(8,128)(2,1)S(1)}, bf16[48,1792]{1,0:T(8,128)(2,1)S(1)}, u32[]{:S(2)}, u32[]{:S(2)}) collective-permute-start(bf16[48,1792]{1,0:T(8,128)(2,1)S(1)} %get-tuple-element.213), channel_id=1, source_target_pairs={{0,1},{1,0},{2,3},{3,2},{4,5},{5,4},{6,7},{7,6},{8,9},{9,8},{10,11... | collective-permute-start | bytes 516104 | tf_op jit(solution)/shard_map/ppermute | solution.py:22
  101.0 17.8 %collective-permute-start.19 = (bf16[96,1920]{1,0:T(8,128)(2,1)S(1)}, bf16[96,1920]{1,0:T(8,128)(2,1)S(1)}, u32[]{:S(2)}, u32[]{:S(2)}) collective-permute-start(bf16[96,1920]{1,0:T(8,128)(2,1)S(1)} %pad_maximum_fusion.9), channel_id=1, source_target_pairs={{0,2},{1,3},{2,0},{3,1},{4,6},{5,7},{6,4},{7,5},{8,10},{9,11},{10,... | collective-permute-start | bytes 1105928 | tf_op jit(solution)/shard_map/ppermute | solution.py:22
  101.4 30.5 %collective-permute-start.21 = (bf16[128,1792]{1,0:T(8,128)(2,1)S(1)}, bf16[128,1792]{1,0:T(8,128)(2,1)S(1)}, u32[]{:S(2)}, u32[]{:S(2)}) collective-permute-start(bf16[128,1792]{1,0:T(8,128)(2,1)S(1)} %convolution_convert_fusion.6), channel_id=1, source_target_pairs={{0,4},{1,5},{2,6},{3,7},{4,0},{5,1},{6,2},{7,3},{8,12},{9,13},{10,... | collective-permute-start | bytes 1376264 | tf_op jit(solution)/shard_map/ppermute | solution.py:22
  103.4 43.6 %collective-permute-start.20 = (bf16[96,3712]{1,0:T(8,128)(2,1)S(1)}, bf16[96,3712]{1,0:T(8,128)(2,1)S(1)}, u32[]{:S(2)}, u32[]{:S(2)}) collective-permute-start(bf16[96,3712]{1,0:T(8,128)(2,1)S(1)} %pad_maximum_fusion.3), channel_id=1, source_target_pairs={{0,2},{1,3},{2,0},{3,1},{4,6},{5,7},{6,4},{7,5},{8,10},{9,11},{10,... | collective-permute-start | bytes 2138120 | tf_op jit(solution)/shard_map/ppermute | solution.py:22
  119.1 27.9 %collective-permute-start.22 = (bf16[128,1920]{1,0:T(8,128)(2,1)S(1)}, bf16[128,1920]{1,0:T(8,128)(2,1)S(1)}, u32[]{:S(2)}, u32[]{:S(2)}) collective-permute-start(bf16[128,1920]{1,0:T(8,128)(2,1)S(1)} %convolution_convert_fusion.5), channel_id=1, source_target_pairs={{0,4},{1,5},{2,6},{3,7},{4,0},{5,1},{6,2},{7,3},{8,12},{9,13},{10,... | collective-permute-start | bytes 1474568 | tf_op jit(solution)/shard_map/ppermute | solution.py:22
  125.7 21.3 %slice-start.1 = ((bf16[192,3712]{1,0:T(8,128)(2,1)}), bf16[48,3712]{1,0:T(8,128)(2,1)S(1)}, s32[]{:S(2)}) async-start(bf16[192,3712]{1,0:T(8,128)(2,1)} %copy-done.3), calls=%async_computation.1 | async-start | bytes 712704 | tf_op jit(solution)/shard_map/slice | solution.py:241
  (7 other events, 17.6 us)
